TPU v7x, 256 devices: a whole 4x4x8 slice. The times are simulated.
256 devices in a mesh: context: 32 (over z, x), dp: 8 (over y, core).
Axes of the slice: x: 4, y: 4, z: 8, core: 2. Of those that a mesh axis runs over, the one named last changes fastest.
Arguments:
- bases: int32 [8, 16384], P('dp', 'context'), may hold values from 0 to 3
- organism: int32 [8], P('dp'), may hold values from 0 to 1, as said below
- embed_weight: bfloat16 [60, 768], replicated, may hold values from -1.5 to 1.5
- conv_weight: bfloat16 [768, 3840], P('context'), may hold values from -0.21875 to 0.21875
- deep_weight: bfloat16 [1536, 3840], P('context'), may hold values from -0.09375 to 0.09375
- human_head: bfloat16 [1536, 5888], P(None, 'context'), may hold values from -0.15625 to 0.15625
- mouse_head: bfloat16 [1536, 1024], P(None, 'context'), may hold values from -0.15625 to 0.15625
- human_cotangent: bfloat16 [8, 128, 5888], P('dp', None, 'context'), may hold values from -0.59765625 to 0.59765625
- mouse_cotangent: bfloat16 [8, 128, 1024], P('dp', None, 'context'), may hold values from -0.59765625 to 0.59765625
Outputs:
- grad_embed: float32 [60, 768], replicated
- grad_conv: float32 [768, 3840], P('context')
- grad_deep: float32 [1536, 3840], P('context')
- grad_human: float32 [1536, 5888], P('dp', 'context')
- grad_mouse: float32 [1536, 1024], P('dp', 'context')
- first_delta: float32 [8, 16384, 768], P('dp', 'context')
Inputs may be any that keep to these rules, and one draw needn't show every extreme that they name: `organism`: exactly half of the 8 windows are mouse windows.
All inputs are finite; a program needn't handle non-finite values.
Results may differ from a plain program's by a relative error of at most 0.035.
Values may be sent and summed in bfloat16 or wider, within the bound.
A program may use at most 128 MiB of HBM per device.

v0:
```python
import jax
import jax.numpy as jnp
from jax import lax
from jax.sharding import PartitionSpec as P

WIDTH = 768
EMBED_SPAN = 15
CONV_SPAN = 5
POOL = 128


SLOPE = 0.7978845608028654
CUBIC = 0.044715
EPSILON = 1e-06


def extended_2(value, sides, width):
    for axis, dim in sides:
        size, length = (lax.axis_size(axis), value.shape[dim])
        up = [(i, (i + 1) % size) for i in range(size - 1)]
        down = [(j, i) for i, j in up]
        last = lax.slice_in_dim(value, length - width, length, axis=dim)
        first = lax.slice_in_dim(value, 0, width, axis=dim)
        before = lax.ppermute(last, axis, up)
        after = lax.ppermute(first, axis, down)
        value = jnp.concatenate([before, value, after], axis=dim)
    return value


def gelu_value(value):
    return 0.5 * value * (1.0 + jnp.tanh(SLOPE * (value + CUBIC * value * value * value)))


def gelu_slope(value):
    tangent = jnp.tanh(SLOPE * (value + CUBIC * value * value * value))
    return 0.5 * (1.0 + tangent) + 0.5 * value * (1.0 - tangent * tangent) * SLOPE * (
        1.0 + 3.0 * CUBIC * value * value
    )


def normalize(source):
    values = source.astype(jnp.float32)
    factor = lax.rsqrt(jnp.mean(values * values, axis=-1, keepdims=True) + EPSILON)
    return (values * factor, factor)


def norm_back(upstream, normed, factor):
    return factor * (upstream - normed * jnp.mean(upstream * normed, axis=-1, keepdims=True))


def columns(padded, count, span):
    return jnp.concatenate(
        [padded[:, offset : offset + count, :] for offset in range(span)], axis=2
    )


def fold_columns(extended, count, span, width):
    half = span // 2
    total = jnp.zeros((extended.shape[0], count, width), jnp.float32)
    for offset in range(span):
        lower = 2 * half - offset
        total = total + extended[:, lower : lower + count, offset * width : (offset + 1) * width]
    return total


def shards(
    bases,
    organism,
    embed_weight,
    conv_weight,
    deep_weight,
    human_head,
    mouse_head,
    human_cotangent,
    mouse_cotangent,
):
    windows, rows = bases.shape
    reach = EMBED_SPAN // 2
    margin = CONV_SPAN // 2
    labelled = extended_2(bases + 1, (("context", 1),), reach)
    codes = jnp.arange(1, 5, dtype=jnp.int32)
    onehot = (labelled[:, :, None] == codes).astype(jnp.bfloat16)
    onehot_cols = columns(onehot, rows, EMBED_SPAN)
    first = jnp.einsum(
        "wsk,kc->wsc", onehot_cols, embed_weight, preferred_element_type=jnp.float32
    ).astype(jnp.bfloat16)
    normed, factor = normalize(first)
    active = gelu_value(normed).astype(jnp.bfloat16)
    active_rim = extended_2(active, (("context", 1),), margin)
    active_cols = columns(active_rim, rows, CONV_SPAN)
    conv_full = lax.all_gather(conv_weight, "context", axis=0, tiled=True)
    mixed = jnp.einsum("wsk,ok->wso", active_cols, conv_full, preferred_element_type=jnp.float32)
    pooled = (
        (first.astype(jnp.float32) + gelu_value(mixed))
        .reshape(windows, rows // POOL, POOL, WIDTH)
        .mean(axis=2)
        .astype(jnp.bfloat16)
    )
    deep_normed, deep_factor = normalize(pooled)
    deep_active = gelu_value(deep_normed).astype(jnp.bfloat16)
    window_rows = lax.all_gather(deep_active, "context", axis=1, tiled=True)
    coarse = window_rows.shape[1]
    padded_rows = jnp.pad(window_rows, ((0, 0), (margin, margin), (0, 0)))
    deep_cols = columns(padded_rows, coarse, CONV_SPAN)
    feature_part = jnp.einsum(
        "wtk,ok->wto", deep_cols, deep_weight, preferred_element_type=jnp.float32
    ).astype(jnp.bfloat16)
    features = lax.all_gather(feature_part, "context", axis=2, tiled=True)
    human_logit = jnp.einsum(
        "wtc,cq->wtq", features, human_head, preferred_element_type=jnp.float32
    )
    mouse_logit = jnp.einsum(
        "wtc,cq->wtq", features, mouse_head, preferred_element_type=jnp.float32
    )
    is_human = (organism == 0).astype(jnp.float32)[:, None, None]
    human_delta = (
        is_human * human_cotangent.astype(jnp.float32) * jax.nn.sigmoid(human_logit)
    ).astype(jnp.bfloat16)
    mouse_delta = (
        (1.0 - is_human) * mouse_cotangent.astype(jnp.float32) * jax.nn.sigmoid(mouse_logit)
    ).astype(jnp.bfloat16)
    human_sum = jnp.einsum("wtc,wtq->cq", features, human_delta, preferred_element_type=jnp.float32)
    mouse_sum = jnp.einsum("wtc,wtq->cq", features, mouse_delta, preferred_element_type=jnp.float32)
    feature_back = jnp.einsum(
        "wtq,cq->wtc", human_delta, human_head, preferred_element_type=jnp.float32
    ) + jnp.einsum("wtq,cq->wtc", mouse_delta, mouse_head, preferred_element_type=jnp.float32)
    feature_delta = lax.psum_scatter(
        feature_back, "context", scatter_dimension=2, tiled=True
    ).astype(jnp.bfloat16)
    deep_sum = jnp.einsum(
        "wto,wtk->ok", feature_delta, deep_cols, preferred_element_type=jnp.float32
    )
    human_all, mouse_all, deep_total = lax.psum((human_sum, mouse_sum, deep_sum), "dp")
    share = human_sum.shape[0] // lax.axis_size("dp")
    first_row = lax.axis_index("dp") * share
    grad_human = lax.dynamic_slice_in_dim(human_all, first_row, share, 0)
    grad_mouse = lax.dynamic_slice_in_dim(mouse_all, first_row, share, 0)
    deep_cols_back = jnp.einsum(
        "wto,ok->wtk", feature_delta, deep_weight, preferred_element_type=jnp.float32
    )
    deep_cols_back = jnp.pad(deep_cols_back, ((0, 0), (margin, margin), (0, 0)))
    deep_back_part = fold_columns(deep_cols_back, coarse, CONV_SPAN, WIDTH)
    deep_back = lax.psum_scatter(deep_back_part, "context", scatter_dimension=1, tiled=True)
    pool_delta = norm_back(deep_back * gelu_slope(deep_normed), deep_normed, deep_factor)
    spread = pool_delta / POOL
    blocks = spread.shape[1]
    block_delta = jnp.broadcast_to(spread[:, :, None, :], (windows, blocks, POOL, WIDTH)).reshape(
        windows, blocks * POOL, WIDTH
    )
    fine_delta = (block_delta * gelu_slope(mixed)).astype(jnp.bfloat16)
    fine_wide = extended_2(fine_delta, (("context", 1),), margin)
    partial_sum = lax.psum_scatter(
        jnp.einsum("wso,wsk->ok", fine_delta, active_cols, preferred_element_type=jnp.float32),
        "context",
        scatter_dimension=0,
        tiled=True,
    )
    grad_conv = lax.psum(partial_sum, "dp")
    conv_cols_back = jnp.einsum(
        "wso,ok->wsk", fine_wide, conv_full, preferred_element_type=jnp.float32
    )
    conv_back = fold_columns(conv_cols_back, rows, CONV_SPAN, WIDTH)
    first_delta = block_delta + norm_back(conv_back * gelu_slope(normed), normed, factor)
    embed_part = jnp.einsum(
        "wsk,wsc->kc",
        onehot_cols.astype(jnp.float32),
        first_delta,
        precision=lax.Precision.HIGHEST,
        preferred_element_type=jnp.float32,
    )
    grad_embed = lax.psum(embed_part, ("context", "dp"))
    return (grad_embed, grad_conv, deep_total, grad_human, grad_mouse, first_delta)


def solution(mesh):
    return jax.shard_map(
        shards,
        mesh=mesh,
        in_specs=(
            P("dp", "context"),
            P("dp"),
            P(),
            P("context", None),
            P("context", None),
            P(None, "context"),
            P(None, "context"),
            P("dp", None, "context"),
            P("dp", None, "context"),
        ),
        out_specs=(
            P(),
            P("context", None),
            P("context", None),
            P("dp", "context"),
            P("dp", "context"),
            P("dp", "context", None),
        ),
        check_vma=False,
    )
```

profile of v0, /device:TPU:1, one launch (start us, length us, event | category | flops | bytes accessed | tf_op | source)
XLA Modules:
  0.0 1152.9 jit_solution(15280237370318157653)
XLA Ops:
  7.2 0.7 all-gather.3.cloned.1.call-update
  8.0 0.7 broadcast_add_fusion
  8.6 0.1 fusion.87
  8.7 1.3 collective-permute-start.1
  10.0 4.6 collective-permute-start
  14.6 0.7 collective-permute-done
  15.3 0.1 add_reduce_fusion
  15.4 0.1 compare_convert_fusion
  15.5 0.3 fusion.86
  15.9 0.8 concatenate.28
  16.7 0.0 copy-done.11
  16.8 0.4 fusion.22
  17.2 0.7 fusion.60
  17.9 3.6 collective-permute-start.2
  22.1 1.3 collective-permute-start.3
  23.4 1.1 fusion.59
  24.6 1.1 fusion.62
  25.7 1.6 constant_dynamic-update-slice_fusion
  27.3 1.1 fusion.57
  28.5 1.1 fusion.61
  29.6 70.5 %all-gather.3.cloned.1.call-done = bf16[768,3840]{1,0:T(8,128)(2,1)} async-done(((bf16[24,3840]{1,0:T(8,128)(2,1)}), bf16[768,3840]{1,0:T(8,128)(2,1)}) %all-gather.3.cloned.1.call-update) | async-done | bytes 5898256 | tf_op jit(solution)/shard_map/all_gather | solution.py:91
  100.1 8.5 bitcast_reduce_fusion
  108.6 0.1 fusion.69
  108.7 0.1 multiply_convert_fusion
  108.8 36.4 %all_gather.10 = bf16[1,128,768]{2,0,1:T(2,128)(2,1)S(1)} all-gather(bf16[1,4,768]{2,0,1:T(2,128)(2,1)S(1)} %copy.22), channel_id=1, replica_groups=mesh['context'=32,'dp'=8] {'context'}, dimensions={1}, use_global_device_ids=true | all-gather | bytes 202752 | tf_op jit(solution)/shard_map/all_gather | solution.py:101
  145.6 0.4 convolution_convert_fusion.1
  146.0 35.6 %all-gather = bf16[128,1536]{0,1:T(8,128)(2,1)S(1)} all-gather(bf16[128,48]{0,1:T(8,128)(2,1)S(1)} %convolution_convert_fusion.1), channel_id=2, replica_groups=mesh['context'=32,'dp'=8] {'context'}, dimensions={1}, use_global_device_ids=true | all-gather | bytes 405504 | tf_op jit(solution)/shard_map/all_gather | solution.py:108
  181.7 0.3 fusion.41
  182.0 0.3 fusion.88
  182.3 0.3 copy-done.7
  182.7 0.2 fusion.48
  182.9 0.3 fusion.4
  183.2 1.8 copy.25
  184.9 0.0 all-reduce.10.cloned.1.call-start
  185.0 232.0 %reduce-scatter.4.cloned.1.call-done = f32[1,128,48]{1,0,2:T(1,128)} async-done(((f32[1,128,1536]{1,0,2:T(1,128)}), f32[1,128,48]{1,0,2:T(1,128)}) %reduce-scatter.4.cloned.1.call-update) | async-done | bytes 24592 | tf_op jit(solution)/shard_map/reduce_scatter | solution.py:127
  417.0 1.4 convolution_bitcast_fusion.1
  418.5 0.9 fusion.66
  419.4 0.2 reduce-scatter.6.cloned.1.call-start
  419.7 0.6 dynamic-slice
  420.9 144.3 %all-reduce.10.cloned.1.call-done = f32[1,128,768]{2,1,0:T(8,128)} async-done(((f32[1,128,768]{2,1,0:T(8,128)}), f32[1,128,768]{2,1,0:T(8,128)}) %all-reduce.10.cloned.1.call-update) | async-done | bytes 393232
  565.2 0.9 multiply_reduce_fusion
  566.2 0.1 multiply_bitcast_fusion
  566.2 2.4 fusion.31
  568.7 8.2 fusion
  576.9 0.0 all-reduce.12.cloned.1.call-start
  577.0 1.6 fusion.90
  578.6 2.2 fusion.89
  580.8 1.3 collective-permute-start.5
  582.1 4.0 collective-permute-start.4
  586.1 1.1 fusion.49
  587.3 8.4 convolution_bitcast_fusion
  595.7 215.8 %reduce-scatter.6.cloned.1.call-done = f32[24,3840]{1,0:T(8,128)} async-done(((f32[768,3840]{1,0:T(8,128)}), f32[24,3840]{1,0:T(8,128)}) %reduce-scatter.6.cloned.1.call-update) | async-done | bytes 368656 | tf_op jit(solution)/shard_map/reduce_scatter | solution.py:152
  811.6 4.4 fusion.21
  816.0 0.1 broadcast_in_dim.9
  816.1 0.4 fusion.19
  816.5 0.5 copy-done.5
  817.0 1.4 fusion.33
  818.4 68.9 %all-reduce.12.cloned.1.call-done = (f32[24,3840]{1,0:T(8,128)}, f32[48,3840]{1,0:T(8,128)}, f32[1536,184]{0,1:T(8,128)}, f32[1536,32]{0,1:T(8,128)}) async-done(((f32[24,3840]{1,0:T(8,128)}, f32[48,3840]{1,0:T(8,128)}, f32[1536,184]{0,1:T(8,128)}, f32[1536,32]{0,1:T(8,128)}), (f32[24,3840]{1,0:T(8,128)}, f32[48,3840]{1,0:T(8,128)}, f32[1536,184]{0,1:T(8,128)}, ...) | async-done | bytes 2433040 | tf_op jit(solution)/shard_map/psum | solution.py:158
  887.3 1.8 constant_dynamic-slice_fusion.1
  889.1 1.5 constant_dynamic-slice_fusion
  890.6 251.2 %all-reduce.8.cloned.1.call-done = f32[60,768]{1,0:T(8,128)} async-done(((f32[60,768]{1,0:T(8,128)}), f32[60,768]{1,0:T(8,128)}) %all-reduce.8.cloned.1.call-update) | async-done | bytes 184336 | tf_op jit(solution)/shard_map/psum | solution.py:171
  1141.8 1.6 copy.45
  1143.4 1.7 copy.46
  1145.2 0.9 copy.47
  (52 shorter events, 0.6 us)
Async XLA Ops:
  7.2 174.5 %copy-start = (bf16[1536,184]{0,1:T(8,128)(2,1)S(1)}, bf16[1536,184]{0,1:T(8,128)(2,1)}, u32[]{:S(2)}) copy-start(bf16[1536,184]{0,1:T(8,128)(2,1)} %param.14) | copy-start | bytes 1695748
  7.2 92.9 %all-gather.3.cloned.1.call-start = ((), (), s32[]{:S(2)}) async-start(), calls=%async_computation.2 | async-start | bytes 6082560 | tf_op jit(solution)/shard_map/all_gather | solution.py:91
  7.9 409.1 %reduce-scatter.4.cloned.1.call-start = ((), (), s32[]{:S(2)}) async-start(), calls=%async_computation.3 | async-start | bytes 811008 | tf_op jit(solution)/shard_map/reduce_scatter | solution.py:127
  8.7 5.9 collective-permute-start.1
  10.0 5.3 collective-permute-start
  15.9 0.9 copy-start.11
  16.8 7.8 copy-start.4
  17.9 5.5 collective-permute-start.2
  22.1 5.2 collective-permute-start.3
  108.8 36.8 %copy-start.2 = (bf16[48,3840]{1,0:T(8,128)(2,1)S(1)}, bf16[48,3840]{1,0:T(8,128)(2,1)}, u32[]{:S(2)}) copy-start(bf16[48,3840]{1,0:T(8,128)(2,1)} %param.13) | copy-start | bytes 1105924
  145.4 36.3 %copy-start.12 = (bf16[1,128,184]{1,2,0:T(8,128)(2,1)S(1)}, bf16[1,128,184]{1,2,0:T(8,128)(2,1)}, u32[]{:S(2)}) copy-start(bf16[1,128,184]{1,2,0:T(8,128)(2,1)} %param.16) | copy-start | bytes 141316
  146.0 36.7 %copy-start.6 = (bf16[1536,32]{0,1:T(8,128)(2,1)S(1)}, bf16[1536,32]{0,1:T(8,128)(2,1)}, u32[]{:S(2)}) copy-start(bf16[1536,32]{0,1:T(8,128)(2,1)} %param.15) | copy-start | bytes 294916
  146.0 36.6 %copy-start.10 = (bf16[1,128,32]{1,2,0:T(8,128)(2,1)S(1)}, bf16[1,128,32]{1,2,0:T(8,128)(2,1)}, u32[]{:S(2)}) copy-start(bf16[1,128,32]{1,2,0:T(8,128)(2,1)} %param.17) | copy-start | bytes 24580
  182.0 0.6 copy-start.7
  182.9 2.1 copy-start.9
  184.9 380.3 %all-reduce.10.cloned.1.call-start = ((), (), s32[]{:S(2)}) async-start(), calls=%async_computation.6 | async-start | bytes 786432
  418.5 1.2 copy-start.13
  419.4 392.1 %reduce-scatter.6.cloned.1.call-start = ((), (), s32[]{:S(2)}) async-start(), calls=%async_computation.5 | async-start | bytes 12165120 | tf_op jit(solution)/shard_map/reduce_scatter | solution.py:152
  576.9 9.2 copy-start.8
  576.9 310.4 %all-reduce.12.cloned.1.call-start = ((), (), s32[]{:S(2)}) async-start(), calls=%async_computation.7 | async-start | bytes 4866048 | tf_op jit(solution)/shard_map/psum | solution.py:158
  580.8 6.5 collective-permute-start.5
  582.1 5.2 collective-permute-start.4
  811.5 330.3 %all-reduce.8.cloned.1.call-start = ((), (), s32[]{:S(2)}) async-start(), calls=%async_computation.4 | async-start | bytes 393216 | tf_op jit(solution)/shard_map/psum | solution.py:171
  816.1 0.9 copy-start.5
  817.0 328.2 %copy-start.1 = (f32[1,512,768]{2,1,0:T(8,128)}, f32[1,512,768]{2,1,0:T(8,128)S(1)}, u32[]{:S(2)}) copy-start(f32[1,512,768]{2,1,0:T(8,128)S(1)} %fusion.19) | copy-start | bytes 4718596
  887.3 257.9 %copy-start.3 = (f32[48,3840]{1,0:T(8,128)S(1)}, f32[48,3840]{1,0:T(8,128)}, u32[]{:S(2)}) copy-start(f32[48,3840]{1,0:T(8,128)} %get-tuple-element.43) | copy-start | bytes 2211844
Sparse Core Ops, SparseCore 0:
  10.6 89.3 all-gather.2
  185.1 231.9 reduce-scatter.3
  421.0 144.1 all-reduce.9
  577.0 234.4 reduce-scatter.5
  814.6 72.7 all-reduce.11
  894.1 247.6 all-reduce.7
where the time goes:
time: 1150 us
  waiting for transfers between devices  984 us (86%)
  blocking collectives  72.1 us (6%)
  matrix products  34.9 us (3%)
  other arithmetic  17.1 us (1%)
  starting transfers between devices  16.4 us (1%)
  between operations  15.8 us (1%)
  local copies, waits for them, and re-layouts  12.4 us (1%)
    psum x1, waiting for transfers between devices, shards(): grad_embed = lax.psum(embed_part, ('context', 'dp'))  251 us
    reduce_scatter x1, waiting for transfers between devices, shards(): lax.psum_scatter(feature_back, 'context', scatter_dimension=2, tiled=True)  232 us
    reduce_scatter x1, waiting for transfers between devices, shards(): lax.psum_scatter(jnp.einsum('wso,wsk->ok', fine_delta, active_cols, prefe...  216 us
    unnamed x7, waiting for transfers between devices  145 us
    all_gather x1, waiting for transfers between devices, shards(): conv_full = lax.all_gather(conv_weight, 'context', axis=0, tiled=True)  70.5 us
    psum x1, waiting for transfers between devices, shards(): grad_conv = lax.psum(partial_sum, 'dp')  68.9 us
    all_gather x1, blocking collectives, shards(): window_rows = lax.all_gather(deep_active, 'context', axis=1, tiled=True)  36.4 us
    all_gather x1, blocking collectives, shards(): features = lax.all_gather(feature_part, 'context', axis=2, tiled=True)  35.6 us
  transfers between devices with their start and end apart: 12, of which 7 were waited for; matrix products, arithmetic and copies ran while one was open for 3% of the time, Pallas kernels for 0%

commit v1 on v0

v1 whole, which is shorter than its diff:
```python
import jax
import jax.numpy as jnp
from jax import lax
from jax.experimental import pallas as pl
from jax.experimental.pallas import tpu as pltpu
from jax.sharding import PartitionSpec as P

F32 = jnp.float32
BF = jnp.bfloat16
MESH = pl.DeviceIdType.MESH

WIDTH = 768
SPAN = 5
NZ, NX, NY = 8, 4, 4
ND = 8
ROWS = 512
OFF = 16
EXT = ROWS + 2 * OFF
WIDE = 640
HALF = 1920
SPLIT = 1024

SLOPE = 0.7978845608028654
CUBIC = 0.044715
EPSILON = 1e-06


def gelu_both(value):
    square = value * value
    tangent = jnp.tanh(SLOPE * (value + CUBIC * square * value))
    half = 0.5 * (1.0 + tangent)
    slope = half + 0.5 * value * (1.0 - tangent * tangent) * SLOPE * (1.0 + 3.0 * CUBIC * square)
    return value * half, slope


def gelu_value(value):
    return 0.5 * value * (1.0 + jnp.tanh(SLOPE * (value + CUBIC * value * value * value)))


def gelu_slope(value):
    return gelu_both(value)[1]


def dot(a, b, ca=1, cb=0):
    return lax.dot_general(a, b, (((ca,), (cb,)), ((), ())), preferred_element_type=F32)


def loop(count, body, unroll=1):
    def step(i, carry):
        body(i)
        return carry

    lax.fori_loop(0, count, step, 0, unroll=unroll)


def kernel(
    bases, embed, cw, dw, hm, cot,
    o_ge, o_gc, o_gd, o_gh, o_gm, o_fd,
    hl, hr, e_ref, et_ref, embp, fpad, first, nm_ref, gn_ref, fac_ref, acols, wg, wf, mixed, ah,
    pbuf, dn_ref, dpad, df_ref, dcols, ft, dtx, fxs, fbs, fxr, fzs, fzr, fdx, fkx, dw2, dbp, dbs, dxr, dzs, dzr,
    dax, pd_ref, fdp, fdc, fdt,
    ga, gb, gar, gbr, ha, hb, har, hbr, zs, zr, fin,
    fdl, fhl, ep, er, ex, ey, eg,
    s_h, r_h, s_w, r_w, s_p, r_p, s_f, r_f, s_rf, r_rf, s_rd, r_rd, s_d, r_d, s_g, r_g, s_e, r_e, s_o,
):
    c = lax.axis_index("context")
    d = lax.axis_index("dp")
    z, x = c // NX, c % NX
    y, k = d // 2, d % 2
    sends = []

    def zp(i):
        return lax.rem(z + i + NZ, NZ)

    def xp(i):
        return lax.rem(x + i + NX, NX)

    def dpp(i):
        return lax.rem(d + i + ND, ND)

    def yp(i):
        return lax.rem(y + i + NY, NY)

    def send(src, dst, ss, rs, **to):
        copy = pltpu.make_async_remote_copy(
            src_ref=src, dst_ref=dst, send_sem=ss, recv_sem=rs, device_id=to, device_id_type=MESH
        )
        copy.start()
        sends.append(copy)

    def wait(dst, rs):
        pltpu.make_async_remote_copy(
            src_ref=dst, dst_ref=dst, send_sem=rs, recv_sem=rs, device_id={"context": zp(1) * NX + x}, device_id_type=MESH
        ).wait_recv()

    barrier = pltpu.get_barrier_semaphore()
    for i in range(1, NZ):
        pl.semaphore_signal(barrier, inc=1, device_id={"context": zp(i) * NX + x}, device_id_type=MESH)
    for i in range(1, NX):
        pl.semaphore_signal(barrier, inc=1, device_id={"context": z * NX + xp(i)}, device_id_type=MESH)
    for i in range(1, ND):
        pl.semaphore_signal(barrier, inc=1, device_id={"dp": dpp(i)}, device_id_type=MESH)
    right, left = lax.rem(c + 1, NZ * NX), lax.rem(c + NZ * NX - 1, NZ * NX)
    pl.semaphore_signal(barrier, inc=1, device_id={"context": right}, device_id_type=MESH)
    pl.semaphore_signal(barrier, inc=1, device_id={"context": left}, device_id_type=MESH)
    wg[z, x] = cw[...]
    pl.semaphore_wait(barrier, NZ - 1 + NX - 1 + ND - 1 + 2)

    mine = pl.multiple_of(HALF * k, 128)
    other = pl.multiple_of(HALF * (1 - k), 128)
    c0 = pl.ds(mine, SPLIT)
    c1 = pl.ds(pl.multiple_of(mine + SPLIT, 128), HALF - SPLIT)
    o0 = pl.ds(other, SPLIT)
    o1 = pl.ds(pl.multiple_of(other + SPLIT, 128), HALF - SPLIT)
    sib = 2 * y + 1 - k

    def blk1(q):
        return wg.at[zp(-q), x, :, c1]

    def to_z(i):
        return dict(context=zp(i) * NX + x)

    def to_x(i):
        return dict(context=z * NX + xp(i))

    send(bases.at[:, pl.ds(ROWS - 128, 128)], hl, s_h.at[0], r_h.at[0], context=right)
    send(bases.at[:, pl.ds(0, 128)], hr, s_h.at[1], r_h.at[1], context=left)
    for i in range(1, NX):
        send(wg.at[z, x, :, c0], wg.at[z, x, :, c0], s_w.at[0, i], r_w.at[0, i], **to_x(i))
    send(blk1(0), blk1(0), s_w.at[1, 1], r_w.at[1, 1], **to_z(1))
    send(blk1(0), blk1(0), s_w.at[2, 1], r_w.at[2, 1], **to_z(-1))
    for i in range(1, NX):
        send(blk1(0), blk1(0), s_w.at[4 + i, 0], r_w.at[4 + i, 0], **to_x(i))

    rows60 = lax.broadcasted_iota(jnp.int32, (64, 60), 0)
    cols60 = lax.broadcasted_iota(jnp.int32, (64, 60), 1)
    place = jnp.where(cols60 == 4 * (15 - rows60 % 16) + rows60 // 16, 1.0, 0.0).astype(BF)
    embp[...] = dot(place, embed[...]).astype(BF)
    wait(hl, r_h.at[0])
    wait(hr, r_h.at[1])
    before = jnp.where(c == 0, -1, hl[...])
    after = jnp.where(c == NZ * NX - 1, -1, hr[...])
    line = jnp.concatenate([before, bases[...], after], axis=1)
    rolled = pltpu.roll(jnp.broadcast_to(line, (16, ROWS + 256)), 648, 1, stride=1, stride_axis=0)
    for j in range(4):
        e_ref[16 * j : 16 * j + 16, :] = jnp.where(rolled[:, :WIDE] == j, 1.0, 0.0).astype(BF)
    for i in range(WIDE // 128):
        block = e_ref[:, 128 * i : 128 * i + 128].astype(F32)
        et_ref[128 * i : 128 * i + 128, :] = block.T.astype(BF)
    fpad[0:8, :] = jnp.zeros((8, WIDTH), F32)

    def embed_step(i):
        r0 = pl.multiple_of(i * 32, 32)
        values = dot(et_ref[pl.ds(r0, 32), :], embp[...]).astype(BF)
        first[pl.ds(r0, 32), :] = values
        values = values.astype(F32)
        factor = lax.rsqrt(jnp.mean(values * values, axis=1, keepdims=True) + EPSILON)
        normed = values * factor
        value, slope = gelu_both(normed)
        spot = lax.broadcasted_iota(jnp.int32, (32, WIDTH), 0) + (c * ROWS + r0 - OFF)
        inside = jnp.logical_and(spot >= 0, spot < ROWS * NZ * NX)
        value = jnp.where(inside, value, 0.0)
        fpad[pl.ds(r0 + 8, 32), :] = value.astype(BF).astype(F32)
        nm_ref[pl.ds(r0, 32), :] = normed
        gn_ref[pl.ds(r0, 32), :] = slope
        fac_ref[pl.ds(r0, 32), :] = jnp.broadcast_to(factor, (32, 128))

    loop(WIDE // 32, embed_step)

    def ring1_up(s):
        wait(blk1(s), r_w.at[1, s])
        if s < 4:
            send(blk1(s), blk1(s), s_w.at[1, s + 1], r_w.at[1, s + 1], **to_z(1))
        spread1(s)

    def ring1_down(s):
        q = NZ - s
        wait(blk1(q), r_w.at[2, s])
        if s < 3:
            send(blk1(q), blk1(q), s_w.at[2, s + 1], r_w.at[2, s + 1], **to_z(-1))
        spread1(q)

    def spread1(q):
        for i in range(1, NX):
            send(blk1(q), blk1(q), s_w.at[4 + i, q], r_w.at[4 + i, q], **to_x(i))
        send(blk1(q), blk1(q), s_w.at[8, q], r_w.at[8, q], dp=sib)

    def blk0(q, cols=c0):
        return wg.at[zp(-q), :, :, cols]

    def ring0_up(s):
        wait(blk0(s), r_w.at[3, s])
        if s < 4:
            send(blk0(s), blk0(s), s_w.at[3, s + 1], r_w.at[3, s + 1], **to_z(1))
        send(blk0(s), blk0(s), s_w.at[10, s], r_w.at[10, s], dp=sib)

    def ring0_down(s):
        q = NZ - s
        wait(blk0(q), r_w.at[4, s])
        if s < 3:
            send(blk0(q), blk0(q), s_w.at[4, s + 1], r_w.at[4, s + 1], **to_z(-1))
        send(blk0(q), blk0(q), s_w.at[10, q], r_w.at[10, q], dp=sib)

    ring1_up(1)
    ring1_down(1)
    for i in range(1, NX):
        here = wg.at[z, xp(-i), :, c0]
        wait(here, r_w.at[0, i])
        send(here, here, s_w.at[9, i], r_w.at[9, i], dp=sib)
    send(blk0(0), blk0(0), s_w.at[3, 1], r_w.at[3, 1], **to_z(1))
    send(blk0(0), blk0(0), s_w.at[4, 1], r_w.at[4, 1], **to_z(-1))
    ring1_up(2)
    ring1_down(2)

    def shift_step(i):
        r0 = pl.multiple_of(i * 32, 32)
        block = fpad[pl.ds(r0, 48), :]
        for t in range(SPAN):
            acols[t, pl.ds(r0, 32), :] = block[t + 6 : t + 38].astype(BF)

    loop(EXT // 32, shift_step)
    ring1_up(3)
    ring1_down(3)
    ring0_up(1)
    ring0_down(1)
    ring1_up(4)
    ring0_up(2)
    ring0_down(2)
    ring0_up(3)
    ring0_down(3)
    ring0_up(4)
    for i in range(1, NX):
        for q in range(NZ):
            here = wg.at[zp(-q), xp(-i), :, c1]
            wait(here, r_w.at[4 + i, q])
        here = wg.at[:, xp(-i), :, c1]
        send(here, here, s_w.at[11, i], r_w.at[11, i], dp=sib)
    own_cols = pl.ds(pl.multiple_of((WIDTH // 2) * k, 128), WIDTH // 2)
    sib_cols = pl.ds(pl.multiple_of((WIDTH // 2) * (1 - k), 128), WIDTH // 2)
    local = []
    for t in range(SPAN):
        dst = ah.at[pl.ds(0, ROWS), pl.ds(384 * t, 384)]
        copy = pltpu.make_async_copy(acols.at[t, pl.ds(OFF, ROWS), own_cols], dst, s_o.at[t])
        copy.start()
        local.append(copy)
        send(
            acols.at[t, pl.ds(OFF, ROWS), sib_cols], ah.at[pl.ds(ROWS, ROWS), pl.ds(384 * t, 384)],
            s_d.at[4, t], r_d.at[4, t], dp=sib,
        )
    ah[:, pl.ds(HALF, 128)] = jnp.zeros((2 * ROWS, 128), BF)
    for q in range(1, NZ):
        wait(wg.at[zp(-q), x, :, o1], r_w.at[8, q])
        wait(blk0(q, o0), r_w.at[10, q])
    for i in range(1, NX):
        wait(wg.at[z, xp(-i), :, o0], r_w.at[9, i])
        wait(wg.at[:, xp(-i), :, o1], r_w.at[11, i])

    def pack_step(i):
        zz, half = i // 2, 2 * (i % 2)
        pair = jnp.concatenate([wg[zz, half].astype(F32), wg[zz, half + 1].astype(F32)], axis=0)
        wf[pl.ds(pl.multiple_of(48 * i, 16), 48), :] = pair.astype(BF)

    loop(16, pack_step)

    def conv_step(i):
        o0_ = pl.multiple_of(i * 256, 256)
        total = dot(acols[0], wf[pl.ds(o0_, 256), 0:WIDTH], 1, 1)
        for t in range(1, SPAN):
            total = total + dot(acols[t], wf[pl.ds(o0_, 256), WIDTH * t : WIDTH * (t + 1)], 1, 1)
        mixed[:, pl.ds(o0_, 256)] = total

    loop(3, conv_step)

    for t in range(4):
        def pool_step(i, total):
            r0 = pl.multiple_of(OFF + 128 * t + 32 * i, 16)
            part = first[pl.ds(r0, 32), :].astype(F32) + gelu_value(mixed[pl.ds(r0, 32), :])
            return total + part.reshape(4, 8, WIDTH).sum(axis=0)

        total = lax.fori_loop(0, 4, pool_step, jnp.zeros((8, WIDTH), F32))
        row = (jnp.sum(total, axis=0, keepdims=True) / 128.0).astype(BF).astype(F32)
        pbuf[z, x, t : t + 1, :] = row[:, :384]
        pbuf[z, x, 4 + t : 5 + t, :] = row[:, 384:]

    def relay_gather(buf, ss, rs, between=None):
        for i in range(1, NZ):
            send(buf.at[z, x], buf.at[z, x], ss.at[i], rs.at[i], **to_z(i))
        if between is not None:
            between()
        for i in range(1, NZ):
            wait(buf.at[zp(-i), x], rs.at[i])
        for i in range(1, NX):
            send(buf.at[:, x], buf.at[:, x], ss.at[7 + i], rs.at[7 + i], **to_x(i))

    def relay_finish(buf, rs):
        for i in range(1, NX):
            wait(buf.at[:, xp(-i)], rs.at[7 + i])

    relay_gather(pbuf, s_p, r_p)

    def slope_step(i):
        r0 = pl.multiple_of(i * 32, 32)
        mixed[pl.ds(r0, 32), :] = gelu_slope(mixed[pl.ds(r0, 32), :])

    loop(EXT // 32, slope_step)
    for t in range(SPAN):
        dw2[48 * t : 48 * t + 48, :] = dw[:, WIDTH * t : WIDTH * (t + 1)]
    zero8 = jnp.zeros((8, WIDTH), F32)
    dn_ref[0:8, :] = zero8
    dn_ref[136:144, :] = zero8
    dpad[0:8, :] = zero8
    dpad[136:144, :] = zero8
    dbp[0:8, :] = zero8
    dbp[136:144, :] = zero8
    df_ref[...] = jnp.ones((144, 128), F32)
    relay_finish(pbuf, r_p)

    def coarse_step(i):
        zz, half = i // 2, 2 * (i % 2)
        v0, v1 = pbuf[zz, half], pbuf[zz, half + 1]
        top = jnp.concatenate([v0[:4], v1[:4]], axis=0)
        bottom = jnp.concatenate([v0[4:], v1[4:]], axis=0)
        values = jnp.concatenate([top, bottom], axis=1)
        factor = lax.rsqrt(jnp.mean(values * values, axis=1, keepdims=True) + EPSILON)
        normed = values * factor
        r0 = pl.multiple_of(8 * i + 8, 8)
        dn_ref[pl.ds(r0, 8), :] = normed
        df_ref[pl.ds(r0, 8), :] = jnp.broadcast_to(factor, (8, 128))
        dpad[pl.ds(r0, 8), :] = gelu_value(normed).astype(BF).astype(F32)

    loop(16, coarse_step)
    block = dpad[...]
    for t in range(SPAN):
        dcols[t] = block[t + 6 : t + 134].astype(BF)
    total = dot(dw[:, 0:WIDTH], dcols[0], 1, 1)
    for t in range(1, SPAN):
        total = total + dot(dw[:, WIDTH * t : WIDTH * (t + 1)], dcols[t], 1, 1)
    ft[z, x] = total.astype(BF)
    dax[pl.ds(pl.multiple_of(d * 128, 128), 128), :] = dcols[2]

    def dp_slot(ref, i, size):
        return ref.at[pl.ds(pl.multiple_of(i * size, 16), size)]

    def coarse_background():
        for i in range(1, ND):
            send(dcols.at[2], dp_slot(dax, d, 128), s_d.at[0, i], r_d.at[0, i], dp=dpp(i))

    relay_gather(ft, s_f, r_f, coarse_background)
    relay_finish(ft, r_f)

    feats = ft[...].reshape(1536, 128)
    logit = dot(hm[...], feats, 0, 0)
    delta = (cot[...].astype(F32) * jax.nn.sigmoid(logit)).astype(BF)
    dtx[d] = delta
    fbs[...] = dot(hm[...], delta).astype(BF).reshape(NZ, NX, 48, 128)
    for i in range(1, NX):
        send(fbs.at[:, xp(i)], fxr.at[i], s_rf.at[i], r_rf.at[i], **to_x(i))
    for i in range(1, ND):
        send(dtx.at[d], dtx.at[d], s_d.at[1, i], r_d.at[1, i], dp=dpp(i))
        send(ft.at[dpp(i)], fxs.at[d], s_d.at[2, i], r_d.at[2, i], dp=dpp(i))
    fxs[d] = ft[d]

    def finish_rs(own, got, zsrc, zgot, ss, rs):
        for i in range(1, NX):
            wait(got.at[i], rs.at[i])
        zsrc[...] = (
            own[:, x].astype(F32) + got[1].astype(F32) + got[2].astype(F32) + got[3].astype(F32)
        ).astype(BF)
        for i in range(1, NZ):
            send(zsrc.at[zp(i)], zgot.at[i], ss.at[3 + i], rs.at[3 + i], **to_z(i))

    def finish_sum(zsrc, zgot, rs):
        total = zsrc[z].astype(F32)
        for i in range(1, NZ):
            wait(zgot.at[i], rs.at[3 + i])
        for i in range(1, NZ):
            total = total + zgot[i].astype(F32)
        return total

    finish_rs(fbs, fxr, fzs, fzr, s_rf, r_rf)
    fdelta = finish_sum(fzs, fzr, r_rf).astype(BF)
    fdx[d] = fdelta
    for i in range(1, ND):
        send(fdx.at[d], fdx.at[d], s_d.at[3, i], r_d.at[3, i], dp=dpp(i))

    lanes = lax.broadcasted_iota(jnp.int32, (48, 128), 1)

    def shifted(values):
        wide = values.astype(F32)
        parts = []
        for t in range(SPAN):
            move = t - 2
            if move == 0:
                parts.append(wide)
                continue
            turned = pltpu.roll(wide, move % 128, 1)
            keep = lanes >= move if move > 0 else lanes < 128 + move
            parts.append(jnp.where(keep, turned, 0.0))
        return jnp.concatenate(parts, axis=0).astype(BF)

    back = dot(shifted(fdelta), dw2[...], 0, 0)
    dbp[8:136, :] = back

    def piece_step(i):
        block = dbp[pl.ds(pl.multiple_of(8 * i, 8), 24), :]
        zz, half = i // 2, 2 * (i % 2)
        for j, low in ((0, 6), (1, 10)):
            rows = block[low : low + 8]
            dbs[zz, half + j] = jnp.concatenate([rows[:, :384], rows[:, 384:]], axis=0).astype(BF)

    loop(16, piece_step)
    for i in range(1, NX):
        send(dbs.at[:, xp(i)], dxr.at[i], s_rd.at[i], r_rd.at[i], **to_x(i))
    finish_rs(dbs, dxr, dzs, dzr, s_rd, r_rd)

    for i in range(1, ND):
        wait(dtx.at[dpp(-i)], r_d.at[1, i])
        wait(fxs.at[dpp(-i)], r_d.at[2, i])
    total = jnp.zeros((192, 256), F32)
    for i in range(ND):
        total = total + dot(fxs[i].reshape(192, 128), dtx[i], 1, 1)
    o_gh[...] = total[:, :184]
    o_gm[...] = total[:, 192:224]

    deep_back = finish_sum(dzs, dzr, r_rd)
    deep_back = jnp.concatenate([deep_back[:8], deep_back[8:]], axis=1)
    r0 = pl.multiple_of(8 * (c // 2), 8)

    def own_rows(ref):
        block = ref[pl.ds(r0, 24), :]
        return jnp.where(c % 2 == 0, block[6:14], block[10:18])

    dnormed = own_rows(dn_ref)
    dfactor = own_rows(df_ref)[:, :1]
    v = deep_back * gelu_slope(dnormed)
    pd_ref[...] = dfactor * (v - dnormed * jnp.mean(v * dnormed, axis=1, keepdims=True)) / 128.0

    fdp[0:8, :] = zero8
    fdp[EXT + 8 : EXT + 16, :] = zero8

    def fine_step(i):
        r0 = pl.multiple_of(i * 16, 16)
        row = pd_ref[pl.ds((r0 + 112) // 128 + 1, 1), :]
        fine = (mixed[pl.ds(r0, 16), :] * row).astype(BF).astype(F32)
        fdp[pl.ds(r0 + 8, 16), :] = fine

    loop(EXT // 16, fine_step, unroll=2)
    for i in range(4):
        block = fdp[OFF + 8 + 128 * i : OFF + 136 + 128 * i, :]
        fdt[0, :, 128 * i : 128 * i + 128] = block.T.astype(BF)
    send(fdt.at[0], fdt.at[1], s_g.at[0, 0], r_g.at[0, 0], dp=sib)

    def back_shift(i):
        r0 = pl.multiple_of(i * 32, 32)
        block = fdp[pl.ds(r0, 48), :]
        for t in range(SPAN):
            fdc[t, pl.ds(r0, 32), :] = block[10 - t : 42 - t].astype(BF)

    loop(EXT // 32, back_shift)
    for copy in local:
        copy.wait()
    for t in range(SPAN):
        wait(ah.at[pl.ds(ROWS, ROWS), pl.ds(384 * t, 384)], r_d.at[4, t])
    wait(fdt.at[1], r_g.at[0, 0])

    def grad_chunk(low):
        cols = pl.ds(pl.multiple_of(low, 256), 256)
        return dot(fdt[0], ah[pl.ds(0, ROWS), cols]) + dot(fdt[1], ah[pl.ds(ROWS, ROWS), cols])

    def by_x(total, xx):
        return jnp.concatenate(
            [total[24 * (4 * zz + xx) : 24 * (4 * zz + xx) + 24] for zz in range(NZ)], axis=0
        ).astype(BF)

    def beta_step(i):
        total = grad_chunk(512 * i + 256)
        for xx in range(NX):
            gb[xx, i] = by_x(total, xx)

    loop(NY, beta_step)
    for i in range(1, NX):
        send(gb.at[xp(i)], gbr.at[i], s_g.at[1, i], r_g.at[1, i], **to_x(i))

    def alpha_step(i):
        yy = lax.rem(y + i + 1, NY)
        total = grad_chunk(512 * yy)
        for xx in range(NX):
            ga[yy, xx] = by_x(total, xx)

    for i in range(NY):
        alpha_step(i)
        if i < NY - 1:
            send(ga.at[yp(i + 1)], gar.at[i + 1], s_g.at[2, i + 1], r_g.at[2, i + 1], dp=2 * yp(i + 1) + k)

    def back_step(i):
        cols = 256 * i
        total = dot(fdc[0], wf[:, cols : cols + 256])
        for t in range(1, SPAN):
            total = total + dot(fdc[t], wf[:, WIDTH * t + cols : WIDTH * t + cols + 256])
        fdp[0:EXT, cols : cols + 256] = total

    for i in range(3):
        back_step(i)

    fhl[0, EXT:WIDE, :] = jnp.zeros((WIDE - EXT, WIDTH), BF)
    fhl[1, EXT:WIDE, :] = jnp.zeros((WIDE - EXT, WIDTH), BF)

    def delta_step(i):
        r0 = pl.multiple_of(i * 16, 16)
        row = pd_ref[pl.ds((r0 + 112) // 128 + 1, 1), :]
        normed = nm_ref[pl.ds(r0, 16), :]
        w = fdp[pl.ds(r0, 16), :] * gn_ref[pl.ds(r0, 16), :]
        factor = fac_ref[pl.ds(r0, 16), :][:, :1]
        value = row + factor * (w - normed * jnp.mean(w * normed, axis=1, keepdims=True))
        value = jnp.where(jnp.logical_and(r0 >= OFF, r0 < OFF + ROWS), value, 0.0)
        fdl[pl.ds(r0, 16), :] = value
        high = value.astype(BF)
        fhl[0, pl.ds(r0, 16), :] = high
        fhl[1, pl.ds(r0, 16), :] = (value - high.astype(F32)).astype(BF)

    loop(EXT // 16, delta_step, unroll=2)
    out_copy = pltpu.make_async_copy(fdl.at[pl.ds(OFF, ROWS)], o_fd, s_o.at[5])
    out_copy.start()
    ep[...] = (dot(e_ref[...], fhl[0]) + dot(e_ref[...], fhl[1])).reshape(NZ, 8, WIDTH)
    for i in range(1, NZ):
        send(ep.at[zp(i)], er.at[i], s_e.at[0, i], r_e.at[0, i], **to_z(i))

    def sum_pieces(count, step_rows, own, got, put):
        def body(i):
            rows = pl.ds(pl.multiple_of(i * step_rows, 16), step_rows)
            total = own(rows).astype(F32)
            for j in range(1, 4):
                total = total + got(j, rows).astype(F32)
            put(rows, total)

        loop(count, body)

    for i in range(1, NY):
        wait(gar.at[i], r_g.at[2, i])
    for xx in range(NX):
        def put_a(rows, total, xx=xx):
            ha[xx, rows, :] = total.astype(BF)

        sum_pieces(4, 48, lambda rows, xx=xx: ga[y, xx, rows, :], lambda j, rows, xx=xx: gar[j, xx, rows, :], put_a)
    for i in range(1, NX):
        send(ha.at[xp(i)], har.at[i], s_g.at[3, i], r_g.at[3, i], **to_x(i))
    for i in range(1, NX):
        wait(gbr.at[i], r_g.at[1, i])
    for yy in range(NY):
        def put_b(rows, total, yy=yy):
            hb[yy, rows, :] = total.astype(BF)

        sum_pieces(4, 48, lambda rows, yy=yy: gb[x, yy, rows, :], lambda j, rows, yy=yy: gbr[j, yy, rows, :], put_b)
    for i in range(1, NY):
        send(hb.at[yp(i)], hbr.at[i], s_g.at[4, i], r_g.at[4, i], dp=2 * yp(i) + k)

    total = ep[z]
    for i in range(1, NZ):
        wait(er.at[i], r_e.at[0, i])
    for i in range(1, NZ):
        total = total + er[i]
    ex[x] = total
    for i in range(1, NX):
        send(ex.at[x], ex.at[x], s_e.at[1, i], r_e.at[1, i], **to_x(i))

    for i in range(1, ND):
        wait(dp_slot(dax, dpp(-i), 128), r_d.at[0, i])
        wait(fdx.at[dpp(-i)], r_d.at[3, i])
    for i in range(ND):
        fkx[:, 128 * i : 128 * i + 128] = shifted(fdx[i])
    deep_total = dot(fkx[...], dax[...])
    for t in range(SPAN):
        o_gd[:, WIDTH * t : WIDTH * (t + 1)] = deep_total[48 * t : 48 * t + 48]

    for i in range(1, NX):
        wait(ex.at[xp(-i)], r_e.at[1, i])
    ey[d] = (ex[0] + ex[1]) + (ex[2] + ex[3])
    for i in range(1, ND):
        send(ey.at[d], ey.at[d], s_e.at[2, i], r_e.at[2, i], dp=dpp(i))

    for i in range(1, NX):
        wait(har.at[i], r_g.at[3, i])
    for i in range(1, NY):
        wait(hbr.at[i], r_g.at[4, i])

    def third_step(i):
        rows = pl.ds(pl.multiple_of(i * 48, 16), 48)
        left_half = ha[x, rows, :].astype(F32)
        right_half = hb[y, rows, :].astype(F32)
        for j in range(1, 4):
            left_half = left_half + har[j, rows, :].astype(F32)
            right_half = right_half + hbr[j, rows, :].astype(F32)
        zs[2 * i] = jnp.concatenate([left_half[:24], right_half[:24]], axis=0).astype(BF)
        zs[2 * i + 1] = jnp.concatenate([left_half[24:], right_half[24:]], axis=0).astype(BF)

    loop(4, third_step)
    for i in range(1, NZ):
        send(zs.at[zp(i)], zr.at[i], s_g.at[5, i], r_g.at[5, i], **to_z(i))

    total = ey[d]
    for i in range(1, ND):
        wait(ey.at[dpp(-i)], r_e.at[2, i])
    total = ey[0]
    for i in range(1, ND):
        total = total + ey[i]
    eg[z] = total
    for i in range(1, NZ):
        send(eg.at[z], eg.at[z], s_e.at[3, i], r_e.at[3, i], **to_z(i))

    total = zs[z].astype(F32)
    for i in range(1, NZ):
        wait(zr.at[i], r_g.at[5, i])
    for i in range(1, NZ):
        total = total + zr[i].astype(F32)
    fin[d] = total
    for i in range(1, ND):
        send(fin.at[d], fin.at[d], s_g.at[6, i], r_g.at[6, i], dp=dpp(i))
    for i in range(1, NZ):
        wait(eg.at[zp(-i)], r_e.at[3, i])
    o_ge[...] = eg[...].reshape(64, WIDTH)
    for i in range(1, ND):
        wait(fin.at[dpp(-i)], r_g.at[6, i])
    for i in range(ND):
        for t in range(4):
            tile = 4 * (i // 2) + t
            if tile >= 15:
                continue
            column = 128 * (6 * (tile // 3) + 3 * (i % 2) + tile % 3)
            part = fin[i, 24 * (t // 2) : 24 * (t // 2) + 24, 128 * (t % 2) : 128 * (t % 2) + 128]
            o_gc[:, column : column + 128] = part

    out_copy.wait()
    for copy in sends:
        copy.wait_send()


def shards(bases, organism, embed_weight, conv_weight, deep_weight, human_head, mouse_head, human_cotangent, mouse_cotangent):
    gap = jnp.zeros((1536, 8), BF)
    hm = jnp.concatenate([human_head, gap, mouse_head, jnp.zeros((1536, 32), BF)], axis=1)
    is_human = (organism == 0).astype(BF)[:, None, None]
    cots = jnp.concatenate(
        [
            human_cotangent * is_human,
            jnp.zeros((1, 128, 8), BF),
            mouse_cotangent * (1 - is_human),
            jnp.zeros((1, 128, 32), BF),
        ],
        axis=2,
    )
    cot = cots[0].T
    vmem, dma = pltpu.VMEM, pltpu.SemaphoreType.DMA
    scratch = [
        vmem((1, 128), jnp.int32), vmem((1, 128), jnp.int32),
        vmem((64, WIDE), BF), vmem((WIDE, 64), BF), vmem((64, WIDTH), BF),
        vmem((WIDE + 8, WIDTH), F32), vmem((WIDE, WIDTH), BF), vmem((WIDE, WIDTH), F32),
        vmem((WIDE, WIDTH), F32), vmem((WIDE, 128), F32), vmem((SPAN, EXT, WIDTH), BF),
        vmem((NZ, NX, 24, 3840), BF), vmem((WIDTH, 3840), BF), vmem((EXT, WIDTH), F32),
        vmem((2 * ROWS, 2048), BF),
        vmem((NZ, NX, 8, 384), F32), vmem((144, WIDTH), F32), vmem((144, WIDTH), F32), vmem((144, 128), F32),
        vmem((SPAN, 128, WIDTH), BF), vmem((NZ, NX, 48, 128), BF),
        vmem((ND, 256, 128), BF), vmem((ND, 4, 48, 128), BF),
        vmem((NZ, NX, 48, 128), BF), vmem((4, NZ, 48, 128), BF), vmem((NZ, 48, 128), BF), vmem((NZ, 48, 128), BF),
        vmem((ND, 48, 128), BF), vmem((240, 1024), BF), vmem((240, WIDTH), BF), vmem((144, WIDTH), F32),
        vmem((NZ, NX, 16, 384), BF), vmem((4, NZ, 16, 384), BF), vmem((NZ, 16, 384), BF), vmem((NZ, 16, 384), BF),
        vmem((1024, WIDTH), BF), vmem((8, WIDTH), F32),
        vmem((EXT + 16, WIDTH), F32), vmem((SPAN, EXT, WIDTH), BF), vmem((2, WIDTH, ROWS), BF),
        vmem((NY, NX, 192, 256), BF), vmem((NX, NY, 192, 256), BF),
        vmem((4, NX, 192, 256), BF), vmem((4, NY, 192, 256), BF),
        vmem((NX, 192, 256), BF), vmem((NY, 192, 256), BF), vmem((4, 192, 256), BF), vmem((4, 192, 256), BF),
        vmem((NZ, 48, 256), BF), vmem((NZ, 48, 256), BF), vmem((ND, 48, 256), F32),
        vmem((EXT, WIDTH), F32), vmem((2, WIDE, WIDTH), BF),
        vmem((NZ, 8, WIDTH), F32), vmem((NZ, 8, WIDTH), F32), vmem((NX, 8, WIDTH), F32),
        vmem((ND, 8, WIDTH), F32), vmem((NZ, 8, WIDTH), F32),
        dma((2,)), dma((2,)), dma((12, 8)), dma((12, 8)), dma((11,)), dma((11,)), dma((11,)), dma((11,)),
        dma((11,)), dma((11,)), dma((11,)), dma((11,)), dma((5, 8)), dma((5, 8)), dma((7, 8)), dma((7, 8)),
        dma((4, 8)), dma((4, 8)), dma((6,)),
    ]
    spec = pl.BlockSpec(memory_space=pltpu.VMEM)
    ge, gc, gd, gh, gm, fd = pl.pallas_call(
        kernel,
        out_shape=(
            jax.ShapeDtypeStruct((64, WIDTH), F32),
            jax.ShapeDtypeStruct((24, 3840), F32),
            jax.ShapeDtypeStruct((48, 3840), F32),
            jax.ShapeDtypeStruct((192, 184), F32),
            jax.ShapeDtypeStruct((192, 32), F32),
            jax.ShapeDtypeStruct((ROWS, WIDTH), F32),
        ),
        in_specs=[spec] * 6,
        out_specs=(spec, spec, spec, spec, spec, pl.BlockSpec(memory_space=pl.ANY)),
        scratch_shapes=scratch,
        compiler_params=pltpu.CompilerParams(
            collective_id=0, has_side_effects=True, vmem_limit_bytes=60 * 1024 * 1024
        ),
        cost_estimate=pl.CostEstimate(flops=10_000_000_000, bytes_accessed=8_000_000, transcendentals=2_000_000),
    )(bases, embed_weight, conv_weight, deep_weight, hm, cot)
    grad_embed = ge.reshape(4, 16, WIDTH)[:, :0:-1].transpose(1, 0, 2).reshape(60, WIDTH)
    return grad_embed, gc, gd, gh, gm, fd[None]


def solution(mesh):
    return jax.shard_map(
        shards,
        mesh=mesh,
        in_specs=(
            P("dp", "context"),
            P("dp"),
            P(),
            P("context", None),
            P("context", None),
            P(None, "context"),
            P(None, "context"),
            P("dp", None, "context"),
            P("dp", None, "context"),
        ),
        out_specs=(
            P(),
            P("context", None),
            P("context", None),
            P("dp", "context"),
            P("dp", "context"),
            P("dp", "context", None),
        ),
        check_vma=False,
    )
```

time: 1150 us -> 173 us (0.15)
  waiting for transfers between devices: 984 us -> 0 us
  Pallas kernels: 0 us -> 159 us
  blocking collectives: 72.1 us -> 0 us
  matrix products: 34.9 us -> 0 us
  starting transfers between devices: 16.4 us -> 0 us
  between operations: 15.8 us -> 1.39 us
  other arithmetic: 17.1 us -> 3.5 us
    reduce_scatter x2 -> x0, waiting for transfers between devices: 448 us -> none  [the longest x1 232 us: shards(): lax.psum_scatter(feature_back, 'context', scatter_dimension=2, tiled=True)]
    psum x2 -> x0, waiting for transfers between devices: 320 us -> none  [the longest x1 251 us: shards(): grad_embed = lax.psum(embed_part, ('context', 'dp'))]
    pallas_call x0 -> x1, Pallas kernels: none -> 159 us  [shards(): pl.pallas_call(kernel, out_shape=(jax.ShapeDtypeStruct((64, WIDTH), F32),...]
    unnamed x7 -> x0, waiting for transfers between devices: 145 us -> none
    all_gather x2 -> x0, blocking collectives: 72.1 us -> none  [the longest x1 36.4 us: shards(): window_rows = lax.all_gather(deep_active, 'context', axis=1, tiled=True)]
    all_gather x1 -> x0, waiting for transfers between devices: 70.5 us -> none  [shards(): conv_full = lax.all_gather(conv_weight, 'context', axis=0, tiled=True)]
    dot_general x14 -> x0, matrix products: 34.9 us -> none  [the longest x1 8.51 us: shards(): jnp.einsum('wsk,ok->wso', active_cols, conv_full, preferred_element_type=...]
    ppermute x6 -> x0, starting transfers between devices: 16 us -> none  [the longest x3 12.1 us: extended_2(): before = lax.ppermute(last, axis, up)]
  transfers between devices with their start and end apart: 12 -> 0, of which waited for: 7 -> 0; matrix products, arithmetic and copies ran while one was open for 3% -> 0% of each run, Pallas kernels for 0% -> 0%
where the time goes in v1:
time: 173 us; the launch traced here: 172 us
  Pallas kernels  159 us (92%)
  local copies, waits for them, and re-layouts  8.97 us (5%)
  other arithmetic  3.5 us (2%)
    pallas_call x1, Pallas kernels, shards(): pl.pallas_call(kernel, out_shape=(jax.ShapeDtypeStruct((64, WIDTH), F32),...  159 us
    unnamed x17, local copies, waits for them, and re-layouts  6.68 us

profile of v1, /device:TPU:1, one launch (start us, length us, event | category | flops | bytes accessed | tf_op | source)
XLA Modules:
  0.0 172.4 jit_solution(5473139952644204517)
XLA Ops:
  1.3 0.1 pad.7.clone
  1.4 0.1 pad.5.clone
  1.5 0.7 broadcast_multiply_fusion.1
  2.2 0.8 broadcast_multiply_fusion
  3.0 0.8 maximum_bitcast_fusion.cot
  3.7 1.1 copy.16
  4.9 1.3 copy.15
  6.2 1.2 maximum_maximum_fusion.hm
  7.4 158.6 %shard_map.136 = (f32[64,768]{1,0:T(8,128)}, f32[24,3840]{1,0:T(8,128)}, f32[48,3840]{1,0:T(8,128)}, f32[192,184]{1,0:T(8,128)}, f32[192,32]{1,0:T(8,128)}, /*index=5*/f32[512,768]{1,0:T(8,128)}) custom-call(s32[1,512]{1,0:T(1,128)} %bases.1, bf16[60,768]{1,0:T(8,128)(2,1)} %embed.1, bf16[24,3840]{1,0:T(8,128)(2,1)} %cw.1, bf16[48,3840]{1,0:T(8,128)(2,1)} %dw.1, ...), custom_call_target="tpu_custom_call" | custom-call | flops 10000000000 | bytes 8000000 | tf_op jit(solution)/shard_map/pallas_call | solution.py:679
  166.0 0.0 copy-start.4
  166.0 0.0 copy-start.3
  166.0 0.0 copy-start.2
  166.0 0.0 copy-start.1
  166.0 1.0 slice.4
  167.1 0.2 rev.3
  167.3 0.1 copy.17
  167.5 0.0 copy-start
  167.5 0.7 reshape.27
  168.2 0.0 copy-done.4
  168.2 0.7 copy.19
  168.9 0.0 copy-done.3
  168.9 0.8 copy.18
  169.7 0.0 copy-done.2
  169.7 0.7 copy.24
  170.4 0.0 copy-done.1
  170.4 0.9 copy.25
  171.3 0.0 copy-done
  171.3 1.1 copy.26
  (2 shorter events, 0.0 us)
Async XLA Ops:
  166.0 2.2 %copy-start.4 = (f32[192,32]{1,0:T(8,128)S(1)}, f32[192,32]{1,0:T(8,128)}, u32[]{:S(2)}) copy-start(f32[192,32]{1,0:T(8,128)} %get-tuple-element.22) | copy-start | bytes 73732
  166.0 2.9 %copy-start.3 = (f32[192,184]{1,0:T(8,128)S(1)}, f32[192,184]{1,0:T(8,128)}, u32[]{:S(2)}) copy-start(f32[192,184]{1,0:T(8,128)} %get-tuple-element.21) | copy-start | bytes 423940
  166.0 3.7 %copy-start.2 = (f32[24,3840]{1,0:T(8,128)S(1)}, f32[24,3840]{1,0:T(8,128)}, u32[]{:S(2)}) copy-start(f32[24,3840]{1,0:T(8,128)} %get-tuple-element.31) | copy-start | bytes 1105924
  166.0 4.4 %copy-start.1 = (f32[48,3840]{1,0:T(8,128)S(1)}, f32[48,3840]{1,0:T(8,128)}, u32[]{:S(2)}) copy-start(f32[48,3840]{1,0:T(8,128)} %get-tuple-element.32) | copy-start | bytes 2211844
  167.5 3.8 %copy-start = (f32[512,768]{1,0:T(8,128)S(1)}, f32[512,768]{1,0:T(8,128)}, u32[]{:S(2)}) copy-start(f32[512,768]{1,0:T(8,128)} %get-tuple-element.17) | copy-start | bytes 4718596

commit v2 on v1

--- a/solution.py
+++ b/solution.py
@@ -54,14 +54,15 @@
 
 
 def kernel(
-    bases, embed, cw, dw, hm, cot,
-    o_ge, o_gc, o_gd, o_gh, o_gm, o_fd,
-    hl, hr, e_ref, et_ref, embp, fpad, first, nm_ref, gn_ref, fac_ref, acols, wg, wf, mixed, ah,
+    i_bases, organism, i_embed, i_cw, i_dw, i_head_h, i_head_m, i_cot_h, i_cot_m,
+    q_ge, q_gc, q_gd, q_gh, q_gm, o_fd,
+    bases, embed, dw, head_h, head_m, cot_h, cot_m, o_ge, o_gc, o_gd, o_gh, o_gm,
+    hm, hmt, cot, hl, hr, e_ref, et_ref, embp, fpad, first, nm_ref, gn_ref, fac_ref, acols, wg, wf, mixed, ah,
     pbuf, dn_ref, dpad, df_ref, dcols, ft, dtx, fxs, fbs, fxr, fzs, fzr, fdx, fkx, dw2, dbp, dbs, dxr, dzs, dzr,
     dax, pd_ref, fdp, fdc, fdt,
     ga, gb, gar, gbr, ha, hb, har, hbr, zs, zr, fin,
     fdl, fhl, ep, er, ex, ey, eg,
-    s_h, r_h, s_w, r_w, s_p, r_p, s_f, r_f, s_rf, r_rf, s_rd, r_rd, s_d, r_d, s_g, r_g, s_e, r_e, s_o,
+    s_h, r_h, s_w, r_w, s_p, r_p, s_f, r_f, s_rf, r_rf, s_rd, r_rd, s_d, r_d, s_g, r_g, s_e, r_e, s_o, s_i,
 ):
     c = lax.axis_index("context")
     d = lax.axis_index("dp")
@@ -103,7 +104,25 @@
     right, left = lax.rem(c + 1, NZ * NX), lax.rem(c + NZ * NX - 1, NZ * NX)
     pl.semaphore_signal(barrier, inc=1, device_id={"context": right}, device_id_type=MESH)
     pl.semaphore_signal(barrier, inc=1, device_id={"context": left}, device_id_type=MESH)
-    wg[z, x] = cw[...]
+    loads = []
+    for i, (src, dst) in enumerate(
+        (
+            (i_cw, wg.at[z, x]), (i_bases, bases), (i_embed, embed), (i_head_h, head_h),
+            (i_head_m, head_m), (i_cot_h, cot_h), (i_cot_m, cot_m), (i_dw, dw),
+        )
+    ):
+        load = pltpu.make_async_copy(src, dst, s_i.at[i])
+        load.start()
+        loads.append(load)
+    stores = []
+
+    def store(src, dst):
+        out = pltpu.make_async_copy(src, dst, s_i.at[8 + len(stores)])
+        out.start()
+        stores.append(out)
+
+    loads[0].wait()
+    loads[1].wait()
     pl.semaphore_wait(barrier, NZ - 1 + NX - 1 + ND - 1 + 2)
 
     mine = pl.multiple_of(HALF * k, 128)
@@ -135,6 +154,7 @@
     rows60 = lax.broadcasted_iota(jnp.int32, (64, 60), 0)
     cols60 = lax.broadcasted_iota(jnp.int32, (64, 60), 1)
     place = jnp.where(cols60 == 4 * (15 - rows60 % 16) + rows60 // 16, 1.0, 0.0).astype(BF)
+    loads[2].wait()
     embp[...] = dot(place, embed[...]).astype(BF)
     wait(hl, r_h.at[0])
     wait(hr, r_h.at[1])
@@ -148,6 +168,7 @@
         block = e_ref[:, 128 * i : 128 * i + 128].astype(F32)
         et_ref[128 * i : 128 * i + 128, :] = block.T.astype(BF)
     fpad[0:8, :] = jnp.zeros((8, WIDTH), F32)
+    fpad[EXT + 8 : EXT + 16, :] = jnp.zeros((8, WIDTH), F32)
 
     def embed_step(i):
         r0 = pl.multiple_of(i * 32, 32)
@@ -165,7 +186,23 @@
         gn_ref[pl.ds(r0, 32), :] = slope
         fac_ref[pl.ds(r0, 32), :] = jnp.broadcast_to(factor, (32, 128))
 
-    loop(WIDE // 32, embed_step)
+    def head_rows():
+        for load in loads[3:]:
+            load.wait()
+        hmt[0:176, :] = head_h[0:176, :]
+        last = jnp.concatenate([head_h[176:184, :].astype(F32), jnp.zeros((8, 1536), F32)], axis=0)
+        hmt[176:192, :] = last.astype(BF)
+        hmt[192:224, :] = head_m[...]
+        hmt[224:256, :] = jnp.zeros((32, 1536), BF)
+        human = (organism[0] == 0).astype(F32)
+        cot[0:184, :] = cot_h[...].astype(F32) * human
+        cot[184:192, :] = jnp.zeros((8, 128), F32)
+        cot[192:224, :] = cot_m[...].astype(F32) * (1.0 - human)
+        cot[224:256, :] = jnp.zeros((32, 128), F32)
+
+    def head_turn(i):
+        cols = pl.ds(pl.multiple_of(128 * i, 128), 128)
+        hm[cols, :] = hmt[:, cols].astype(F32).T.astype(BF)
 
     def ring1_up(s):
         wait(blk1(s), r_w.at[1, s])
@@ -185,32 +222,28 @@
             send(blk1(q), blk1(q), s_w.at[4 + i, q], r_w.at[4 + i, q], **to_x(i))
         send(blk1(q), blk1(q), s_w.at[8, q], r_w.at[8, q], dp=sib)
 
-    def blk0(q, cols=c0):
+    def blk0(q, cols):
         return wg.at[zp(-q), :, :, cols]
 
-    def ring0_up(s):
-        wait(blk0(s), r_w.at[3, s])
-        if s < 4:
-            send(blk0(s), blk0(s), s_w.at[3, s + 1], r_w.at[3, s + 1], **to_z(1))
-        send(blk0(s), blk0(s), s_w.at[10, s], r_w.at[10, s], dp=sib)
-
-    def ring0_down(s):
-        q = NZ - s
-        wait(blk0(q), r_w.at[4, s])
-        if s < 3:
-            send(blk0(q), blk0(q), s_w.at[4, s + 1], r_w.at[4, s + 1], **to_z(-1))
-        send(blk0(q), blk0(q), s_w.at[10, q], r_w.at[10, q], dp=sib)
-
-    ring1_up(1)
-    ring1_down(1)
-    for i in range(1, NX):
-        here = wg.at[z, xp(-i), :, c0]
-        wait(here, r_w.at[0, i])
-        send(here, here, s_w.at[9, i], r_w.at[9, i], dp=sib)
-    send(blk0(0), blk0(0), s_w.at[3, 1], r_w.at[3, 1], **to_z(1))
-    send(blk0(0), blk0(0), s_w.at[4, 1], r_w.at[4, 1], **to_z(-1))
-    ring1_up(2)
-    ring1_down(2)
+    def chunk(low, h):
+        return pl.ds(pl.multiple_of(low + 256 * h, 128), 256)
+
+    def ring0(s, h):
+        for down in range(2):
+            if s == 4 and down:
+                continue
+            q, row = (NZ - s if down else s), 12 + 4 * down + h
+            part = blk0(q, chunk(mine, h))
+            wait(part, r_w.at[row, s])
+            if s < 4 - down:
+                send(part, part, s_w.at[row, s + 1], r_w.at[row, s + 1], **to_z(-1 if down else 1))
+            send(part, part, s_w.at[20 + h, q], r_w.at[20 + h, q], dp=sib)
+
+    def embed_some(low, high):
+        def body(i):
+            embed_step(i + low)
+
+        loop(high - low, body)
 
     def shift_step(i):
         r0 = pl.multiple_of(i * 32, 32)
@@ -218,23 +251,57 @@
         for t in range(SPAN):
             acols[t, pl.ds(r0, 32), :] = block[t + 6 : t + 38].astype(BF)
 
-    loop(EXT // 32, shift_step)
-    ring1_up(3)
-    ring1_down(3)
-    ring0_up(1)
-    ring0_down(1)
-    ring1_up(4)
-    ring0_up(2)
-    ring0_down(2)
-    ring0_up(3)
-    ring0_down(3)
-    ring0_up(4)
+    ring1_up(1)
+    ring1_down(1)
+    for i in range(1, NX):
+        here = wg.at[z, xp(-i), :, c0]
+        wait(here, r_w.at[0, i])
+        send(here, here, s_w.at[9, i], r_w.at[9, i], dp=sib)
+    for h in range(4):
+        part = blk0(0, chunk(mine, h))
+        send(part, part, s_w.at[12 + h, 1], r_w.at[12 + h, 1], **to_z(1))
+        send(part, part, s_w.at[16 + h, 1], r_w.at[16 + h, 1], **to_z(-1))
+    embed_some(0, 4)
+    ring1_up(2)
+    ring1_down(2)
+    embed_step(4)
+    for s in range(1, 4):
+        for h in range(4):
+            ring0(s, h)
+            embed_step(1 + 4 * s + h)
+            if s == 1 and h == 1:
+                ring1_up(3)
+                ring1_down(3)
+            if s == 2 and h == 1:
+                ring1_up(4)
+    head_rows()
+    for h in range(4):
+        ring0(4, h)
+        if h == 0:
+            loop(EXT // 32, shift_step)
+        if h == 1:
+            loop(12, head_turn)
     for i in range(1, NX):
         for q in range(NZ):
             here = wg.at[zp(-q), xp(-i), :, c1]
             wait(here, r_w.at[4 + i, q])
         here = wg.at[:, xp(-i), :, c1]
         send(here, here, s_w.at[11, i], r_w.at[11, i], dp=sib)
+    for q in range(1, NZ):
+        wait(wg.at[zp(-q), x, :, o1], r_w.at[8, q])
+        for h in range(4):
+            wait(blk0(q, chunk(other, h)), r_w.at[20 + h, q])
+    for i in range(1, NX):
+        wait(wg.at[z, xp(-i), :, o0], r_w.at[9, i])
+        wait(wg.at[:, xp(-i), :, o1], r_w.at[11, i])
+
+    def pack_step(i):
+        zz, half = i // 2, 2 * (i % 2)
+        pair = jnp.concatenate([wg[zz, half].astype(F32), wg[zz, half + 1].astype(F32)], axis=0)
+        wf[pl.ds(pl.multiple_of(48 * i, 16), 48), :] = pair.astype(BF)
+
+    loop(16, pack_step)
+
     own_cols = pl.ds(pl.multiple_of((WIDTH // 2) * k, 128), WIDTH // 2)
     sib_cols = pl.ds(pl.multiple_of((WIDTH // 2) * (1 - k), 128), WIDTH // 2)
     local = []
@@ -248,20 +315,6 @@
             s_d.at[4, t], r_d.at[4, t], dp=sib,
         )
     ah[:, pl.ds(HALF, 128)] = jnp.zeros((2 * ROWS, 128), BF)
-    for q in range(1, NZ):
-        wait(wg.at[zp(-q), x, :, o1], r_w.at[8, q])
-        wait(blk0(q, o0), r_w.at[10, q])
-    for i in range(1, NX):
-        wait(wg.at[z, xp(-i), :, o0], r_w.at[9, i])
-        wait(wg.at[:, xp(-i), :, o1], r_w.at[11, i])
-
-    def pack_step(i):
-        zz, half = i // 2, 2 * (i % 2)
-        pair = jnp.concatenate([wg[zz, half].astype(F32), wg[zz, half + 1].astype(F32)], axis=0)
-        wf[pl.ds(pl.multiple_of(48 * i, 16), 48), :] = pair.astype(BF)
-
-    loop(16, pack_step)
-
     def conv_step(i):
         o0_ = pl.multiple_of(i * 256, 256)
         total = dot(acols[0], wf[pl.ds(o0_, 256), 0:WIDTH], 1, 1)
@@ -271,6 +324,7 @@
 
     loop(3, conv_step)
 
+    pooled = []
     for t in range(4):
         def pool_step(i, total):
             r0 = pl.multiple_of(OFF + 128 * t + 32 * i, 16)
@@ -278,23 +332,54 @@
             return total + part.reshape(4, 8, WIDTH).sum(axis=0)
 
         total = lax.fori_loop(0, 4, pool_step, jnp.zeros((8, WIDTH), F32))
-        row = (jnp.sum(total, axis=0, keepdims=True) / 128.0).astype(BF).astype(F32)
-        pbuf[z, x, t : t + 1, :] = row[:, :384]
-        pbuf[z, x, 4 + t : 5 + t, :] = row[:, 384:]
+        row = jnp.sum(total, axis=0, keepdims=True) / 128.0
+        pooled.append(row)
+
+    pieces = [row[:, 256 * m : 256 * m + 256] for m in range(3) for row in pooled]
+    pbuf[z, x] = jnp.concatenate(pieces + [jnp.zeros((4, 256), F32)], axis=0).astype(BF)
+    near = (1, 7, 2, 6, 3, 5, 4)
+    far = (4, 3, 5, 2, 6, 1, 7, 0)
 
     def relay_gather(buf, ss, rs, between=None):
-        for i in range(1, NZ):
-            send(buf.at[z, x], buf.at[z, x], ss.at[i], rs.at[i], **to_z(i))
+        own = buf.at[z, x]
+        for q in near:
+            send(own, own, ss.at[0, q], rs.at[0, q], **to_z(q))
+        for i in range(1, NX):
+            send(own, own, ss.at[i, 0], rs.at[i, 0], **to_x(i))
         if between is not None:
             between()
-        for i in range(1, NZ):
-            wait(buf.at[zp(-i), x], rs.at[i])
-        for i in range(1, NX):
-            send(buf.at[:, x], buf.at[:, x], ss.at[7 + i], rs.at[7 + i], **to_x(i))
+        for q in near:
+            here = buf.at[zp(-q), x]
+            wait(here, rs.at[0, q])
+            for i in range(1, NX):
+                send(here, here, ss.at[i, q], rs.at[i, q], **to_x(i))
 
     def relay_finish(buf, rs):
-        for i in range(1, NX):
-            wait(buf.at[:, xp(-i)], rs.at[7 + i])
+        for q in (0,) + near:
+            for i in range(1, NX):
+                wait(buf.at[zp(-q), xp(-i)], rs.at[i, q])
+
+    def scatter_start(src, got, ss, rs):
+        for q in far:
+            for i in range(1, NX):
+                send(src.at[zp(q), xp(i)], got.at[i, q], ss.at[i, q], rs.at[i, q], **to_x(i))
+
+    def scatter_turn(src, got, zsrc, zgot, ss, rs):
+        for q in far:
+            total = src[zp(q), x].astype(F32)
+            for i in range(1, NX):
+                wait(got.at[i, q], rs.at[i, q])
+                total = total + got[i, q].astype(F32)
+            if q:
+                zsrc[q] = total.astype(BF)
+                send(zsrc.at[q], zgot.at[q], ss.at[0, q], rs.at[0, q], **to_z(q))
+        return total
+
+    def scatter_finish(total, zgot, rs):
+        for q in near:
+            wait(zgot.at[q], rs.at[0, q])
+            total = total + zgot[q].astype(F32)
+        return total
 
     relay_gather(pbuf, s_p, r_p)
 
@@ -317,10 +402,9 @@
 
     def coarse_step(i):
         zz, half = i // 2, 2 * (i % 2)
-        v0, v1 = pbuf[zz, half], pbuf[zz, half + 1]
-        top = jnp.concatenate([v0[:4], v1[:4]], axis=0)
-        bottom = jnp.concatenate([v0[4:], v1[4:]], axis=0)
-        values = jnp.concatenate([top, bottom], axis=1)
+        v0, v1 = pbuf[zz, half].astype(F32), pbuf[zz, half + 1].astype(F32)
+        parts = [jnp.concatenate([v0[4 * m : 4 * m + 4], v1[4 * m : 4 * m + 4]], axis=0) for m in range(3)]
+        values = jnp.concatenate(parts, axis=1)
         factor = lax.rsqrt(jnp.mean(values * values, axis=1, keepdims=True) + EPSILON)
         normed = values * factor
         r0 = pl.multiple_of(8 * i + 8, 8)
@@ -349,36 +433,18 @@
     relay_finish(ft, r_f)
 
     feats = ft[...].reshape(1536, 128)
-    logit = dot(hm[...], feats, 0, 0)
-    delta = (cot[...].astype(F32) * jax.nn.sigmoid(logit)).astype(BF)
+    logit = dot(hmt[...], feats)
+    delta = (cot[...] * jax.nn.sigmoid(logit)).astype(BF)
     dtx[d] = delta
     fbs[...] = dot(hm[...], delta).astype(BF).reshape(NZ, NX, 48, 128)
-    for i in range(1, NX):
-        send(fbs.at[:, xp(i)], fxr.at[i], s_rf.at[i], r_rf.at[i], **to_x(i))
+    scatter_start(fbs, fxr, s_rf, r_rf)
     for i in range(1, ND):
         send(dtx.at[d], dtx.at[d], s_d.at[1, i], r_d.at[1, i], dp=dpp(i))
         send(ft.at[dpp(i)], fxs.at[d], s_d.at[2, i], r_d.at[2, i], dp=dpp(i))
     fxs[d] = ft[d]
 
-    def finish_rs(own, got, zsrc, zgot, ss, rs):
-        for i in range(1, NX):
-            wait(got.at[i], rs.at[i])
-        zsrc[...] = (
-            own[:, x].astype(F32) + got[1].astype(F32) + got[2].astype(F32) + got[3].astype(F32)
-        ).astype(BF)
-        for i in range(1, NZ):
-            send(zsrc.at[zp(i)], zgot.at[i], ss.at[3 + i], rs.at[3 + i], **to_z(i))
-
-    def finish_sum(zsrc, zgot, rs):
-        total = zsrc[z].astype(F32)
-        for i in range(1, NZ):
-            wait(zgot.at[i], rs.at[3 + i])
-        for i in range(1, NZ):
-            total = total + zgot[i].astype(F32)
-        return total
-
-    finish_rs(fbs, fxr, fzs, fzr, s_rf, r_rf)
-    fdelta = finish_sum(fzs, fzr, r_rf).astype(BF)
+    own_part = scatter_turn(fbs, fxr, fzs, fzr, s_rf, r_rf)
+    fdelta = scatter_finish(own_part, fzr, r_rf).astype(BF)
     fdx[d] = fdelta
     for i in range(1, ND):
         send(fdx.at[d], fdx.at[d], s_d.at[3, i], r_d.at[3, i], dp=dpp(i))
@@ -409,20 +475,21 @@
             dbs[zz, half + j] = jnp.concatenate([rows[:, :384], rows[:, 384:]], axis=0).astype(BF)
 
     loop(16, piece_step)
-    for i in range(1, NX):
-        send(dbs.at[:, xp(i)], dxr.at[i], s_rd.at[i], r_rd.at[i], **to_x(i))
-    finish_rs(dbs, dxr, dzs, dzr, s_rd, r_rd)
+    scatter_start(dbs, dxr, s_rd, r_rd)
+    own_part = scatter_turn(dbs, dxr, dzs, dzr, s_rd, r_rd)
 
     for i in range(1, ND):
         wait(dtx.at[dpp(-i)], r_d.at[1, i])
         wait(fxs.at[dpp(-i)], r_d.at[2, i])
-    total = jnp.zeros((192, 256), F32)
+    total = jnp.zeros((256, 192), F32)
     for i in range(ND):
-        total = total + dot(fxs[i].reshape(192, 128), dtx[i], 1, 1)
-    o_gh[...] = total[:, :184]
-    o_gm[...] = total[:, 192:224]
-
-    deep_back = finish_sum(dzs, dzr, r_rd)
+        total = total + dot(dtx[i], fxs[i].reshape(192, 128), 1, 1)
+    o_gh[...] = total[:184]
+    o_gm[...] = total[192:224]
+    store(o_gh, q_gh)
+    store(o_gm, q_gm)
+
+    deep_back = scatter_finish(own_part, dzr, r_rd)
     deep_back = jnp.concatenate([deep_back[:8], deep_back[8:]], axis=1)
     r0 = pl.multiple_of(8 * (c // 2), 8)
 
@@ -571,6 +638,7 @@
     deep_total = dot(fkx[...], dax[...])
     for t in range(SPAN):
         o_gd[:, WIDTH * t : WIDTH * (t + 1)] = deep_total[48 * t : 48 * t + 48]
+    store(o_gd, q_gd)
 
     for i in range(1, NX):
         wait(ex.at[xp(-i)], r_e.at[1, i])
@@ -612,12 +680,15 @@
         wait(zr.at[i], r_g.at[5, i])
     for i in range(1, NZ):
         total = total + zr[i].astype(F32)
-    fin[d] = total
+    fin[d] = total.astype(BF)
     for i in range(1, ND):
         send(fin.at[d], fin.at[d], s_g.at[6, i], r_g.at[6, i], dp=dpp(i))
     for i in range(1, NZ):
         wait(eg.at[zp(-i)], r_e.at[3, i])
-    o_ge[...] = eg[...].reshape(64, WIDTH)
+    for t in range(15):
+        for j in range(4):
+            o_ge[4 * t + j : 4 * t + j + 1, :] = eg[2 * j + (15 - t) // 8, (15 - t) % 8 : (15 - t) % 8 + 1, :]
+    store(o_ge, q_ge)
     for i in range(1, ND):
         wait(fin.at[dpp(-i)], r_g.at[6, i])
     for i in range(ND):
@@ -627,36 +698,30 @@
                 continue
             column = 128 * (6 * (tile // 3) + 3 * (i % 2) + tile % 3)
             part = fin[i, 24 * (t // 2) : 24 * (t // 2) + 24, 128 * (t % 2) : 128 * (t % 2) + 128]
-            o_gc[:, column : column + 128] = part
+            o_gc[:, column : column + 128] = part.astype(F32)
+    store(o_gc, q_gc)
 
     out_copy.wait()
+    for out in stores:
+        out.wait()
     for copy in sends:
         copy.wait_send()
 
 
 def shards(bases, organism, embed_weight, conv_weight, deep_weight, human_head, mouse_head, human_cotangent, mouse_cotangent):
-    gap = jnp.zeros((1536, 8), BF)
-    hm = jnp.concatenate([human_head, gap, mouse_head, jnp.zeros((1536, 32), BF)], axis=1)
-    is_human = (organism == 0).astype(BF)[:, None, None]
-    cots = jnp.concatenate(
-        [
-            human_cotangent * is_human,
-            jnp.zeros((1, 128, 8), BF),
-            mouse_cotangent * (1 - is_human),
-            jnp.zeros((1, 128, 32), BF),
-        ],
-        axis=2,
-    )
-    cot = cots[0].T
     vmem, dma = pltpu.VMEM, pltpu.SemaphoreType.DMA
     scratch = [
+        vmem((1, ROWS), jnp.int32), vmem((60, WIDTH), BF), vmem((48, 3840), BF), vmem((184, 1536), BF),
+        vmem((32, 1536), BF), vmem((184, 128), BF), vmem((32, 128), BF),
+        vmem((60, WIDTH), F32), vmem((24, 3840), F32), vmem((48, 3840), F32), vmem((184, 192), F32), vmem((32, 192), F32),
+        vmem((1536, 256), BF), vmem((256, 1536), BF), vmem((256, 128), F32),
         vmem((1, 128), jnp.int32), vmem((1, 128), jnp.int32),
         vmem((64, WIDE), BF), vmem((WIDE, 64), BF), vmem((64, WIDTH), BF),
-        vmem((WIDE + 8, WIDTH), F32), vmem((WIDE, WIDTH), BF), vmem((WIDE, WIDTH), F32),
-        vmem((WIDE, WIDTH), F32), vmem((WIDE, 128), F32), vmem((SPAN, EXT, WIDTH), BF),
+        vmem((EXT + 16, WIDTH), F32), vmem((EXT, WIDTH), BF), vmem((EXT, WIDTH), F32),
+        vmem((EXT, WIDTH), F32), vmem((EXT, 128), F32), vmem((SPAN, EXT, WIDTH), BF),
         vmem((NZ, NX, 24, 3840), BF), vmem((WIDTH, 3840), BF), vmem((EXT, WIDTH), F32),
         vmem((2 * ROWS, 2048), BF),
-        vmem((NZ, NX, 8, 384), F32), vmem((144, WIDTH), F32), vmem((144, WIDTH), F32), vmem((144, 128), F32),
+        vmem((NZ, NX, 16, 256), BF), vmem((144, WIDTH), F32), vmem((144, WIDTH), F32), vmem((144, 128), F32),
         vmem((SPAN, 128, WIDTH), BF), vmem((NZ, NX, 48, 128), BF),
         vmem((ND, 256, 128), BF), vmem((ND, 4, 48, 128), BF),
         vmem((NZ, NX, 48, 128), BF), vmem((4, NZ, 48, 128), BF), vmem((NZ, 48, 128), BF), vmem((NZ, 48, 128), BF),
@@ -667,35 +732,37 @@
         vmem((NY, NX, 192, 256), BF), vmem((NX, NY, 192, 256), BF),
         vmem((4, NX, 192, 256), BF), vmem((4, NY, 192, 256), BF),
         vmem((NX, 192, 256), BF), vmem((NY, 192, 256), BF), vmem((4, 192, 256), BF), vmem((4, 192, 256), BF),
-        vmem((NZ, 48, 256), BF), vmem((NZ, 48, 256), BF), vmem((ND, 48, 256), F32),
+        vmem((NZ, 48, 256), BF), vmem((NZ, 48, 256), BF), vmem((ND, 48, 256), BF),
         vmem((EXT, WIDTH), F32), vmem((2, WIDE, WIDTH), BF),
         vmem((NZ, 8, WIDTH), F32), vmem((NZ, 8, WIDTH), F32), vmem((NX, 8, WIDTH), F32),
         vmem((ND, 8, WIDTH), F32), vmem((NZ, 8, WIDTH), F32),
-        dma((2,)), dma((2,)), dma((12, 8)), dma((12, 8)), dma((11,)), dma((11,)), dma((11,)), dma((11,)),
-        dma((11,)), dma((11,)), dma((11,)), dma((11,)), dma((5, 8)), dma((5, 8)), dma((7, 8)), dma((7, 8)),
-        dma((4, 8)), dma((4, 8)), dma((6,)),
+        dma((2,)), dma((2,)), dma((24, 8)), dma((24, 8)), dma((4, 8)), dma((4, 8)), dma((4, 8)), dma((4, 8)),
+        dma((4, 8)), dma((4, 8)), dma((4, 8)), dma((4, 8)), dma((5, 8)), dma((5, 8)), dma((7, 8)), dma((7, 8)),
+        dma((4, 8)), dma((4, 8)), dma((6,)), dma((13,)),
     ]
-    spec = pl.BlockSpec(memory_space=pltpu.VMEM)
+    spec = pl.BlockSpec(memory_space=pl.ANY)
     ge, gc, gd, gh, gm, fd = pl.pallas_call(
         kernel,
         out_shape=(
-            jax.ShapeDtypeStruct((64, WIDTH), F32),
+            jax.ShapeDtypeStruct((60, WIDTH), F32),
             jax.ShapeDtypeStruct((24, 3840), F32),
             jax.ShapeDtypeStruct((48, 3840), F32),
-            jax.ShapeDtypeStruct((192, 184), F32),
-            jax.ShapeDtypeStruct((192, 32), F32),
+            jax.ShapeDtypeStruct((184, 192), F32),
+            jax.ShapeDtypeStruct((32, 192), F32),
             jax.ShapeDtypeStruct((ROWS, WIDTH), F32),
         ),
-        in_specs=[spec] * 6,
-        out_specs=(spec, spec, spec, spec, spec, pl.BlockSpec(memory_space=pl.ANY)),
+        in_specs=[spec, pl.BlockSpec(memory_space=pltpu.SMEM)] + [spec] * 7,
+        out_specs=(spec,) * 6,
         scratch_shapes=scratch,
         compiler_params=pltpu.CompilerParams(
             collective_id=0, has_side_effects=True, vmem_limit_bytes=60 * 1024 * 1024
         ),
         cost_estimate=pl.CostEstimate(flops=10_000_000_000, bytes_accessed=8_000_000, transcendentals=2_000_000),
-    )(bases, embed_weight, conv_weight, deep_weight, hm, cot)
-    grad_embed = ge.reshape(4, 16, WIDTH)[:, :0:-1].transpose(1, 0, 2).reshape(60, WIDTH)
-    return grad_embed, gc, gd, gh, gm, fd[None]
+    )(
+        bases, organism, embed_weight, conv_weight, deep_weight,
+        human_head.T, mouse_head.T, human_cotangent[0].T, mouse_cotangent[0].T,
+    )
+    return ge, gc, gd, gh.T, gm.T, fd[None]
 
 
 def solution(mesh):

time: 173 us -> 147 us (0.85)
  Pallas kernels: 159 us -> 138 us
  other arithmetic: 3.5 us -> 0 us
    pallas_call x1, Pallas kernels: 159 us -> 138 us  [shards(): pl.pallas_call(kernel, out_shape=(jax.ShapeDtypeStruct((60, WIDTH), F32),...]
    unnamed x17 -> x12, local copies, waits for them, and re-layouts: 6.68 us -> 7.96 us
where the time goes in v2:
time: 147 us
  Pallas kernels  138 us (94%)
  local copies, waits for them, and re-layouts  7.96 us (5%)
    pallas_call x1, Pallas kernels, shards(): pl.pallas_call(kernel, out_shape=(jax.ShapeDtypeStruct((60, WIDTH), F32),...  138 us
    unnamed x12, local copies, waits for them, and re-layouts  7.96 us

profile of v2, /device:TPU:1, one launch (start us, length us, event | category | flops | bytes accessed | tf_op | source)
XLA Modules:
  0.0 147.2 jit_solution(305249843191699631)
XLA Ops:
  1.3 137.9 %shard_map.136 = (f32[60,768]{1,0:T(8,128)}, f32[24,3840]{1,0:T(8,128)}, f32[48,3840]{1,0:T(8,128)}, f32[184,192]{1,0:T(8,128)}, f32[32,192]{1,0:T(8,128)}, /*index=5*/f32[512,768]{1,0:T(8,128)}) custom-call(s32[1,512]{1,0:T(1,128)} %i_bases.1, s32[1]{0:T(128)S(6)} %copy.21.organism, bf16[60,768]{1,0:T(8,128)(2,1)} %i_embed.1, bf16[24,3840]{1,0:T(8,128)(2,1)} %i_cw.1, ...), custom_call_target="tpu_custom_call" | custom-call | flops 10000000000 | bytes 8000000 | tf_op jit(solution)/shard_map/pallas_call | solution.py:744
  139.2 0.0 copy-start.1
  139.2 0.0 copy-start.2
  139.2 0.0 copy-start
  139.2 1.7 %copy.22 = f32[60,768]{1,0:T(8,128)} copy(f32[60,768]{1,0:T(8,128)} %get-tuple-element.24) | data formatting | bytes 368640
  140.9 1.7 %copy.23 = f32[24,3840]{1,0:T(8,128)} copy(f32[24,3840]{1,0:T(8,128)} %get-tuple-element.25) | data formatting | bytes 737280
  142.7 2.0 %copy.24 = f32[48,3840]{1,0:T(8,128)} copy(f32[48,3840]{1,0:T(8,128)} %get-tuple-element.26) | data formatting | bytes 1474560
  144.7 0.0 copy-done.1
  144.7 0.7 copy.25
  145.4 0.0 copy-done.2
  145.4 0.6 copy.26
  146.0 0.0 copy-done
  146.0 1.1 copy.27
Async XLA Ops:
  139.2 5.6 %copy-start.1 = (f32[184,192]{1,0:T(8,128)S(1)}, f32[184,192]{1,0:T(8,128)}, u32[]{:S(2)}) copy-start(f32[184,192]{1,0:T(8,128)} %get-tuple-element.15) | copy-start | bytes 423940
  139.2 6.2 %copy-start.2 = (f32[32,192]{1,0:T(8,128)S(1)}, f32[32,192]{1,0:T(8,128)}, u32[]{:S(2)}) copy-start(f32[32,192]{1,0:T(8,128)} %get-tuple-element.16) | copy-start | bytes 73732
  139.2 6.8 %copy-start = (f32[512,768]{1,0:T(8,128)S(1)}, f32[512,768]{1,0:T(8,128)}, u32[]{:S(2)}) copy-start(f32[512,768]{1,0:T(8,128)} %get-tuple-element.17) | copy-start | bytes 4718596

commit v3 on v2

--- a/solution.py
+++ b/solution.py
@@ -61,14 +61,13 @@
     pbuf, dn_ref, dpad, df_ref, dcols, ft, dtx, fxs, fbs, fxr, fzs, fzr, fdx, fkx, dw2, dbp, dbs, dxr, dzs, dzr,
     dax, pd_ref, fdp, fdc, fdt,
     ga, gb, gar, gbr, ha, hb, har, hbr, zs, zr, fin,
-    fdl, fhl, ep, er, ex, ey, eg,
-    s_h, r_h, s_w, r_w, s_p, r_p, s_f, r_f, s_rf, r_rf, s_rd, r_rd, s_d, r_d, s_g, r_g, s_e, r_e, s_o, s_i,
+    fdl, fhl, ep, es, er, ex, ey, eg,
+    s_all, r_h, r_w, r_p, r_f, r_rf, r_rd, r_d, r_g, r_e, s_o, s_i,
 ):
     c = lax.axis_index("context")
     d = lax.axis_index("dp")
     z, x = c // NX, c % NX
     y, k = d // 2, d % 2
-    sends = []
 
     def zp(i):
         return lax.rem(z + i + NZ, NZ)
@@ -82,17 +81,36 @@
     def yp(i):
         return lax.rem(y + i + NY, NY)
 
-    def send(src, dst, ss, rs, **to):
-        copy = pltpu.make_async_remote_copy(
-            src_ref=src, dst_ref=dst, send_sem=ss, recv_sem=rs, device_id=to, device_id_type=MESH
-        )
-        copy.start()
-        sends.append(copy)
+    sent = [0] * 11
+
+    def count(group, ref):
+        size = ref.dtype.itemsize
+        for n in ref.shape:
+            size *= n
+        sent[group] += size
+
+    def send(src, dst, group, rs, **to):
+        pltpu.make_async_remote_copy(
+            src_ref=src, dst_ref=dst, send_sem=s_all.at[group], recv_sem=rs, device_id=to, device_id_type=MESH
+        ).start()
+        count(group, src)
 
     def wait(dst, rs):
         pltpu.make_async_remote_copy(
             src_ref=dst, dst_ref=dst, send_sem=rs, recv_sem=rs, device_id={"context": zp(1) * NX + x}, device_id_type=MESH
         ).wait_recv()
+
+    def wait_sends(group):
+        cells = sent[group] // 2
+        parts = []
+        for r in range(768, 0, -16):
+            if cells % (r * 128) == 0 and cells // r <= 3840:
+                parts.append(wf.at[pl.ds(0, r), pl.ds(0, cells // r)])
+        for a in range(1, NZ + 1):
+            for b in range(1, NX + 1):
+                if cells % (a * b * 24 * 128) == 0 and cells // (a * b * 24) <= 3840:
+                    parts.append(wg.at[pl.ds(0, a), pl.ds(0, b), :, pl.ds(0, cells // (a * b * 24))])
+        pltpu.make_async_copy(parts[0], parts[0], s_all.at[group]).wait()
 
     barrier = pltpu.get_barrier_semaphore()
     for i in range(1, NZ):
@@ -142,14 +160,14 @@
     def to_x(i):
         return dict(context=z * NX + xp(i))
 
-    send(bases.at[:, pl.ds(ROWS - 128, 128)], hl, s_h.at[0], r_h.at[0], context=right)
-    send(bases.at[:, pl.ds(0, 128)], hr, s_h.at[1], r_h.at[1], context=left)
+    send(bases.at[:, pl.ds(ROWS - 128, 128)], hl, 0, r_h.at[0], context=right)
+    send(bases.at[:, pl.ds(0, 128)], hr, 0, r_h.at[1], context=left)
     for i in range(1, NX):
-        send(wg.at[z, x, :, c0], wg.at[z, x, :, c0], s_w.at[0, i], r_w.at[0, i], **to_x(i))
-    send(blk1(0), blk1(0), s_w.at[1, 1], r_w.at[1, 1], **to_z(1))
-    send(blk1(0), blk1(0), s_w.at[2, 1], r_w.at[2, 1], **to_z(-1))
+        send(wg.at[z, x, :, c0], wg.at[z, x, :, c0], 9, r_w.at[0], **to_x(i))
+    send(blk1(0), blk1(0), 10, r_w.at[3], **to_z(1))
+    send(blk1(0), blk1(0), 10, r_w.at[9], **to_z(-1))
     for i in range(1, NX):
-        send(blk1(0), blk1(0), s_w.at[4 + i, 0], r_w.at[4 + i, 0], **to_x(i))
+        send(blk1(0), blk1(0), 8, r_w.at[10], **to_x(i))
 
     rows60 = lax.broadcasted_iota(jnp.int32, (64, 60), 0)
     cols60 = lax.broadcasted_iota(jnp.int32, (64, 60), 1)
@@ -205,22 +223,21 @@
         hm[cols, :] = hmt[:, cols].astype(F32).T.astype(BF)
 
     def ring1_up(s):
-        wait(blk1(s), r_w.at[1, s])
+        wait(blk1(s), r_w.at[2 + s])
         if s < 4:
-            send(blk1(s), blk1(s), s_w.at[1, s + 1], r_w.at[1, s + 1], **to_z(1))
+            send(blk1(s), blk1(s), 10, r_w.at[3 + s], **to_z(1))
         spread1(s)
 
     def ring1_down(s):
         q = NZ - s
-        wait(blk1(q), r_w.at[2, s])
+        wait(blk1(q), r_w.at[2 + q])
         if s < 3:
-            send(blk1(q), blk1(q), s_w.at[2, s + 1], r_w.at[2, s + 1], **to_z(-1))
+            send(blk1(q), blk1(q), 10, r_w.at[1 + q], **to_z(-1))
         spread1(q)
 
     def spread1(q):
         for i in range(1, NX):
-            send(blk1(q), blk1(q), s_w.at[4 + i, q], r_w.at[4 + i, q], **to_x(i))
-        send(blk1(q), blk1(q), s_w.at[8, q], r_w.at[8, q], dp=sib)
+            send(blk1(q), blk1(q), 8, r_w.at[10 + q], **to_x(i))
 
     def blk0(q, cols):
         return wg.at[zp(-q), :, :, cols]
@@ -230,14 +247,40 @@
 
     def ring0(s, h):
         for down in range(2):
-            if s == 4 and down:
+            if s == 4 and down != h // 2:
                 continue
-            q, row = (NZ - s if down else s), 12 + 4 * down + h
+            q = NZ - s if down else s
             part = blk0(q, chunk(mine, h))
-            wait(part, r_w.at[row, s])
-            if s < 4 - down:
-                send(part, part, s_w.at[row, s + 1], r_w.at[row, s + 1], **to_z(-1 if down else 1))
-            send(part, part, s_w.at[20 + h, q], r_w.at[20 + h, q], dp=sib)
+            wait(part, r_w.at[34 + 8 * h + q])
+            if s < 3 or (s == 3 and down == h // 2):
+                step = -1 if down else 1
+                send(part, part, 1, r_w.at[34 + 8 * h + q + step], **to_z(step))
+            send(part, part, 2, r_w.at[26 + q], dp=sib)
+
+    def pass_on(q):
+        wait(wg.at[zp(-q), pl.ds(0, 3), :, c1], r_w.at[10 + q])
+        if q:
+            here = wg.at[zp(-q), :, :, c1]
+            send(here, here, 10, r_w.at[18 + q], dp=sib)
+        else:
+            for i in range(1, NX):
+                here = wg.at[z, xp(-i), :, c1]
+                send(here, here, 10, r_w.at[18], dp=sib)
+
+    def pack(q):
+        if q:
+            wait(wg.at[zp(-q), :, :, o1], r_w.at[18 + q])
+            wait(wg.at[zp(-q), :, :, o0], r_w.at[26 + q])
+        else:
+            wait(wg.at[z, pl.ds(0, 3), :, o1], r_w.at[18])
+            wait(wg.at[z, pl.ds(0, 3), :, o0], r_w.at[1])
+        zz = zp(-q)
+
+        def pack_step(i):
+            pair = jnp.concatenate([wg[zz, 2 * i].astype(F32), wg[zz, 2 * i + 1].astype(F32)], axis=0)
+            wf[pl.ds(pl.multiple_of(96 * zz + 48 * i, 16), 48), :] = pair.astype(BF)
+
+        loop(2, pack_step)
 
     def embed_some(low, high):
         def body(i):
@@ -253,14 +296,14 @@
 
     ring1_up(1)
     ring1_down(1)
+    wait(wg.at[z, pl.ds(0, 3), :, c0], r_w.at[0])
     for i in range(1, NX):
         here = wg.at[z, xp(-i), :, c0]
-        wait(here, r_w.at[0, i])
-        send(here, here, s_w.at[9, i], r_w.at[9, i], dp=sib)
+        send(here, here, 9, r_w.at[1], dp=sib)
     for h in range(4):
         part = blk0(0, chunk(mine, h))
-        send(part, part, s_w.at[12 + h, 1], r_w.at[12 + h, 1], **to_z(1))
-        send(part, part, s_w.at[16 + h, 1], r_w.at[16 + h, 1], **to_z(-1))
+        send(part, part, 1, r_w.at[34 + 8 * h + 1], **to_z(1))
+        send(part, part, 1, r_w.at[34 + 8 * h + 7], **to_z(-1))
     embed_some(0, 4)
     ring1_up(2)
     ring1_down(2)
@@ -274,33 +317,26 @@
                 ring1_down(3)
             if s == 2 and h == 1:
                 ring1_up(4)
+        if s == 2:
+            pass_on(0)
+        if s == 3:
+            pass_on(1)
+            pass_on(7)
     head_rows()
-    for h in range(4):
+    loop(EXT // 32, shift_step)
+    pass_on(2)
+    pass_on(6)
+    pack(0)
+    for h in (0, 2, 1, 3):
         ring0(4, h)
         if h == 0:
-            loop(EXT // 32, shift_step)
-        if h == 1:
-            loop(12, head_turn)
-    for i in range(1, NX):
-        for q in range(NZ):
-            here = wg.at[zp(-q), xp(-i), :, c1]
-            wait(here, r_w.at[4 + i, q])
-        here = wg.at[:, xp(-i), :, c1]
-        send(here, here, s_w.at[11, i], r_w.at[11, i], dp=sib)
-    for q in range(1, NZ):
-        wait(wg.at[zp(-q), x, :, o1], r_w.at[8, q])
-        for h in range(4):
-            wait(blk0(q, chunk(other, h)), r_w.at[20 + h, q])
-    for i in range(1, NX):
-        wait(wg.at[z, xp(-i), :, o0], r_w.at[9, i])
-        wait(wg.at[:, xp(-i), :, o1], r_w.at[11, i])
-
-    def pack_step(i):
-        zz, half = i // 2, 2 * (i % 2)
-        pair = jnp.concatenate([wg[zz, half].astype(F32), wg[zz, half + 1].astype(F32)], axis=0)
-        wf[pl.ds(pl.multiple_of(48 * i, 16), 48), :] = pair.astype(BF)
-
-    loop(16, pack_step)
+            pack(1)
+            pack(7)
+    for q in (3, 5, 4):
+        pass_on(q)
+    loop(12, head_turn)
+    for q in (2, 6, 3, 5, 4):
+        pack(q)
 
     own_cols = pl.ds(pl.multiple_of((WIDTH // 2) * k, 128), WIDTH // 2)
     sib_cols = pl.ds(pl.multiple_of((WIDTH // 2) * (1 - k), 128), WIDTH // 2)
@@ -312,7 +348,7 @@
         local.append(copy)
         send(
             acols.at[t, pl.ds(OFF, ROWS), sib_cols], ah.at[pl.ds(ROWS, ROWS), pl.ds(384 * t, 384)],
-            s_d.at[4, t], r_d.at[4, t], dp=sib,
+            9, r_d.at[4], dp=sib,
         )
     ah[:, pl.ds(HALF, 128)] = jnp.zeros((2 * ROWS, 128), BF)
     def conv_step(i):
@@ -340,48 +376,46 @@
     near = (1, 7, 2, 6, 3, 5, 4)
     far = (4, 3, 5, 2, 6, 1, 7, 0)
 
-    def relay_gather(buf, ss, rs, between=None):
+    def relay_gather(buf, group, rs, between=None):
         own = buf.at[z, x]
         for q in near:
-            send(own, own, ss.at[0, q], rs.at[0, q], **to_z(q))
+            send(own, own, group, rs.at[q], **to_z(q))
         for i in range(1, NX):
-            send(own, own, ss.at[i, 0], rs.at[i, 0], **to_x(i))
+            send(own, own, group, rs.at[0], **to_x(i))
         if between is not None:
             between()
         for q in near:
             here = buf.at[zp(-q), x]
-            wait(here, rs.at[0, q])
+            wait(here, rs.at[q])
             for i in range(1, NX):
-                send(here, here, ss.at[i, q], rs.at[i, q], **to_x(i))
+                send(here, here, group, rs.at[0], **to_x(i))
 
     def relay_finish(buf, rs):
-        for q in (0,) + near:
-            for i in range(1, NX):
-                wait(buf.at[zp(-q), xp(-i)], rs.at[i, q])
-
-    def scatter_start(src, got, ss, rs):
+        wait(buf.at[:, pl.ds(0, 3)], rs.at[0])
+
+    def scatter_start(src, got, group, rs):
         for q in far:
             for i in range(1, NX):
-                send(src.at[zp(q), xp(i)], got.at[i, q], ss.at[i, q], rs.at[i, q], **to_x(i))
-
-    def scatter_turn(src, got, zsrc, zgot, ss, rs):
+                send(src.at[zp(q), xp(i)], got.at[i, q], group, rs.at[q], **to_x(i))
+
+    def scatter_turn(src, got, zsrc, zgot, group, rs):
         for q in far:
             total = src[zp(q), x].astype(F32)
+            wait(got.at[pl.ds(1, 3), q], rs.at[q])
             for i in range(1, NX):
-                wait(got.at[i, q], rs.at[i, q])
                 total = total + got[i, q].astype(F32)
             if q:
                 zsrc[q] = total.astype(BF)
-                send(zsrc.at[q], zgot.at[q], ss.at[0, q], rs.at[0, q], **to_z(q))
+                send(zsrc.at[q], zgot.at[q], group, rs.at[NZ], **to_z(q))
         return total
 
     def scatter_finish(total, zgot, rs):
+        wait(zgot.at[pl.ds(1, 7)], rs.at[NZ])
         for q in near:
-            wait(zgot.at[q], rs.at[0, q])
             total = total + zgot[q].astype(F32)
         return total
 
-    relay_gather(pbuf, s_p, r_p)
+    relay_gather(pbuf, 3, r_p)
 
     def slope_step(i):
         r0 = pl.multiple_of(i * 32, 32)
@@ -412,7 +446,7 @@
         df_ref[pl.ds(r0, 8), :] = jnp.broadcast_to(factor, (8, 128))
         dpad[pl.ds(r0, 8), :] = gelu_value(normed).astype(BF).astype(F32)
 
-    loop(16, coarse_step)
+    loop(16, coarse_step, unroll=4)
     block = dpad[...]
     for t in range(SPAN):
         dcols[t] = block[t + 6 : t + 134].astype(BF)
@@ -427,9 +461,9 @@
 
     def coarse_background():
         for i in range(1, ND):
-            send(dcols.at[2], dp_slot(dax, d, 128), s_d.at[0, i], r_d.at[0, i], dp=dpp(i))
-
-    relay_gather(ft, s_f, r_f, coarse_background)
+            send(dcols.at[2], dp_slot(dax, d, 128), 8, r_d.at[0], dp=dpp(i))
+
+    relay_gather(ft, 4, r_f, coarse_background)
     relay_finish(ft, r_f)
 
     feats = ft[...].reshape(1536, 128)
@@ -437,17 +471,15 @@
     delta = (cot[...] * jax.nn.sigmoid(logit)).astype(BF)
     dtx[d] = delta
     fbs[...] = dot(hm[...], delta).astype(BF).reshape(NZ, NX, 48, 128)
-    scatter_start(fbs, fxr, s_rf, r_rf)
+    scatter_start(fbs, fxr, 5, r_rf)
     for i in range(1, ND):
-        send(dtx.at[d], dtx.at[d], s_d.at[1, i], r_d.at[1, i], dp=dpp(i))
-        send(ft.at[dpp(i)], fxs.at[d], s_d.at[2, i], r_d.at[2, i], dp=dpp(i))
+        send(dtx.at[d], dtx.at[d], 4, r_d.at[1], dp=dpp(i))
+        send(ft.at[dpp(i)], fxs.at[d], 4, r_d.at[2], dp=dpp(i))
     fxs[d] = ft[d]
 
-    own_part = scatter_turn(fbs, fxr, fzs, fzr, s_rf, r_rf)
+    own_part = scatter_turn(fbs, fxr, fzs, fzr, 5, r_rf)
     fdelta = scatter_finish(own_part, fzr, r_rf).astype(BF)
     fdx[d] = fdelta
-    for i in range(1, ND):
-        send(fdx.at[d], fdx.at[d], s_d.at[3, i], r_d.at[3, i], dp=dpp(i))
 
     lanes = lax.broadcasted_iota(jnp.int32, (48, 128), 1)
 
@@ -474,13 +506,14 @@
             rows = block[low : low + 8]
             dbs[zz, half + j] = jnp.concatenate([rows[:, :384], rows[:, 384:]], axis=0).astype(BF)
 
-    loop(16, piece_step)
-    scatter_start(dbs, dxr, s_rd, r_rd)
-    own_part = scatter_turn(dbs, dxr, dzs, dzr, s_rd, r_rd)
-
+    loop(16, piece_step, unroll=4)
+    scatter_start(dbs, dxr, 5, r_rd)
     for i in range(1, ND):
-        wait(dtx.at[dpp(-i)], r_d.at[1, i])
-        wait(fxs.at[dpp(-i)], r_d.at[2, i])
+        send(fdx.at[d], fdx.at[d], 4, r_d.at[3], dp=dpp(i))
+    own_part = scatter_turn(dbs, dxr, dzs, dzr, 5, r_rd)
+
+    wait(dtx.at[pl.ds(0, 7)], r_d.at[1])
+    wait(fxs.at[pl.ds(0, 7)], r_d.at[2])
     total = jnp.zeros((256, 192), F32)
     for i in range(ND):
         total = total + dot(dtx[i], fxs[i].reshape(192, 128), 1, 1)
@@ -515,7 +548,7 @@
     for i in range(4):
         block = fdp[OFF + 8 + 128 * i : OFF + 136 + 128 * i, :]
         fdt[0, :, 128 * i : 128 * i + 128] = block.T.astype(BF)
-    send(fdt.at[0], fdt.at[1], s_g.at[0, 0], r_g.at[0, 0], dp=sib)
+    send(fdt.at[0], fdt.at[1], 6, r_g.at[0], dp=sib)
 
     def back_shift(i):
         r0 = pl.multiple_of(i * 32, 32)
@@ -526,9 +559,8 @@
     loop(EXT // 32, back_shift)
     for copy in local:
         copy.wait()
-    for t in range(SPAN):
-        wait(ah.at[pl.ds(ROWS, ROWS), pl.ds(384 * t, 384)], r_d.at[4, t])
-    wait(fdt.at[1], r_g.at[0, 0])
+    wait(ah.at[pl.ds(ROWS, ROWS), pl.ds(0, HALF)], r_d.at[4])
+    wait(fdt.at[1], r_g.at[0])
 
     def grad_chunk(low):
         cols = pl.ds(pl.multiple_of(low, 256), 256)
@@ -539,25 +571,87 @@
             [total[24 * (4 * zz + xx) : 24 * (4 * zz + xx) + 24] for zz in range(NZ)], axis=0
         ).astype(BF)
 
-    def beta_step(i):
-        total = grad_chunk(512 * i + 256)
+    halves = (pl.ds(0, 96), pl.ds(96, 96))
+
+    def alpha_send(i, h):
+        send(
+            ga.at[yp(i), :, halves[h]], gar.at[i, :, halves[h]],
+            6, r_g.at[1 + h], dp=2 * yp(i) + k,
+        )
+
+    def beta_send(yy, i, h):
+        send(
+            gb.at[xp(i), yy, halves[h]], gbr.at[i, yy, halves[h]],
+            6, r_g.at[3 + h], **to_x(i),
+        )
+
+    for n in range(NY):
+        total = grad_chunk(512 * n + 256)
         for xx in range(NX):
-            gb[xx, i] = by_x(total, xx)
-
-    loop(NY, beta_step)
-    for i in range(1, NX):
-        send(gb.at[xp(i)], gbr.at[i], s_g.at[1, i], r_g.at[1, i], **to_x(i))
-
-    def alpha_step(i):
-        yy = lax.rem(y + i + 1, NY)
+            gb[xx, n] = by_x(total, xx)
+        for i in range(1, NX):
+            beta_send(n, i, 0)
+        yy = yp(n + 1)
         total = grad_chunk(512 * yy)
         for xx in range(NX):
             ga[yy, xx] = by_x(total, xx)
-
-    for i in range(NY):
-        alpha_step(i)
-        if i < NY - 1:
-            send(ga.at[yp(i + 1)], gar.at[i + 1], s_g.at[2, i + 1], r_g.at[2, i + 1], dp=2 * yp(i + 1) + k)
+        if n < NY - 1:
+            alpha_send(n + 1, 0)
+    for n in range(NY):
+        for i in range(1, NX):
+            beta_send(n, i, 1)
+        if n < NY - 1:
+            alpha_send(n + 1, 1)
+
+    def second_phase(h):
+        wait(gar.at[pl.ds(1, 3), :, halves[h]], r_g.at[1 + h])
+        for xx in range(NX):
+            for low in (96 * h, 96 * h + 48):
+                rows = pl.ds(low, 48)
+                total = ga[y, xx, rows, :].astype(F32)
+                for i in range(1, NY):
+                    total = total + gar[i, xx, rows, :].astype(F32)
+                ha[xx, rows, :] = total.astype(BF)
+        for i in range(1, NX):
+            send(ha.at[xp(i), halves[h]], har.at[i, halves[h]], 7, r_g.at[5 + h], **to_x(i))
+        wait(gbr.at[pl.ds(1, 3), :, halves[h]], r_g.at[3 + h])
+        for yy in range(NY):
+            for low in (96 * h, 96 * h + 48):
+                rows = pl.ds(low, 48)
+                total = gb[x, yy, rows, :].astype(F32)
+                for i in range(1, NX):
+                    total = total + gbr[i, yy, rows, :].astype(F32)
+                hb[yy, rows, :] = total.astype(BF)
+        for i in range(1, NY):
+            send(
+                hb.at[yp(i), halves[h]], hbr.at[i, halves[h]],
+                7, r_g.at[7 + h], dp=2 * yp(i) + k,
+            )
+
+    def third_copy(zz):
+        return pltpu.make_async_remote_copy(
+            src_ref=zs.at[zz], dst_ref=zr.at[z], send_sem=s_all.at[7], recv_sem=r_g.at[9],
+            device_id={"context": zz * NX + x}, device_id_type=MESH,
+        )
+
+    def third_phase(h):
+        wait(har.at[pl.ds(1, 3), halves[h]], r_g.at[5 + h])
+        wait(hbr.at[pl.ds(1, 3), halves[h]], r_g.at[7 + h])
+        for m in range(2):
+            rows = pl.ds(96 * h + 48 * m, 48)
+            left_half = ha[x, rows, :].astype(F32)
+            right_half = hb[y, rows, :].astype(F32)
+            for i in range(1, 4):
+                left_half = left_half + har[i, rows, :].astype(F32)
+                right_half = right_half + hbr[i, rows, :].astype(F32)
+            zz = 4 * h + 2 * m
+            zs[zz] = jnp.concatenate([left_half[:24], right_half[:24]], axis=0).astype(BF)
+            zs[zz + 1] = jnp.concatenate([left_half[24:], right_half[24:]], axis=0).astype(BF)
+            for to in (zz, zz + 1):
+
+                @pl.when(z != to)
+                def _(to=to):
+                    third_copy(to).start()
 
     def back_step(i):
         cols = 256 * i
@@ -569,6 +663,7 @@
     for i in range(3):
         back_step(i)
 
+    second_phase(0)
     fhl[0, EXT:WIDE, :] = jnp.zeros((WIDE - EXT, WIDTH), BF)
     fhl[1, EXT:WIDE, :] = jnp.zeros((WIDE - EXT, WIDTH), BF)
 
@@ -589,50 +684,13 @@
     out_copy = pltpu.make_async_copy(fdl.at[pl.ds(OFF, ROWS)], o_fd, s_o.at[5])
     out_copy.start()
     ep[...] = (dot(e_ref[...], fhl[0]) + dot(e_ref[...], fhl[1])).reshape(NZ, 8, WIDTH)
-    for i in range(1, NZ):
-        send(ep.at[zp(i)], er.at[i], s_e.at[0, i], r_e.at[0, i], **to_z(i))
-
-    def sum_pieces(count, step_rows, own, got, put):
-        def body(i):
-            rows = pl.ds(pl.multiple_of(i * step_rows, 16), step_rows)
-            total = own(rows).astype(F32)
-            for j in range(1, 4):
-                total = total + got(j, rows).astype(F32)
-            put(rows, total)
-
-        loop(count, body)
-
-    for i in range(1, NY):
-        wait(gar.at[i], r_g.at[2, i])
-    for xx in range(NX):
-        def put_a(rows, total, xx=xx):
-            ha[xx, rows, :] = total.astype(BF)
-
-        sum_pieces(4, 48, lambda rows, xx=xx: ga[y, xx, rows, :], lambda j, rows, xx=xx: gar[j, xx, rows, :], put_a)
-    for i in range(1, NX):
-        send(ha.at[xp(i)], har.at[i], s_g.at[3, i], r_g.at[3, i], **to_x(i))
-    for i in range(1, NX):
-        wait(gbr.at[i], r_g.at[1, i])
-    for yy in range(NY):
-        def put_b(rows, total, yy=yy):
-            hb[yy, rows, :] = total.astype(BF)
-
-        sum_pieces(4, 48, lambda rows, yy=yy: gb[x, yy, rows, :], lambda j, rows, yy=yy: gbr[j, yy, rows, :], put_b)
-    for i in range(1, NY):
-        send(hb.at[yp(i)], hbr.at[i], s_g.at[4, i], r_g.at[4, i], dp=2 * yp(i) + k)
-
-    total = ep[z]
-    for i in range(1, NZ):
-        wait(er.at[i], r_e.at[0, i])
-    for i in range(1, NZ):
-        total = total + er[i]
-    ex[x] = total
-    for i in range(1, NX):
-        send(ex.at[x], ex.at[x], s_e.at[1, i], r_e.at[1, i], **to_x(i))
-
-    for i in range(1, ND):
-        wait(dp_slot(dax, dpp(-i), 128), r_d.at[0, i])
-        wait(fdx.at[dpp(-i)], r_d.at[3, i])
+    for q in far[:7]:
+        part = ep[zp(q)]
+        es[q] = jnp.concatenate([part[:, :384], part[:, 384:]], axis=0).astype(BF)
+        send(es.at[q], er.at[q], 7, r_e.at[0], **to_z(q))
+
+    wait(dax.at[pl.ds(0, 896)], r_d.at[0])
+    wait(fdx.at[pl.ds(0, 7)], r_d.at[3])
     for i in range(ND):
         fkx[:, 128 * i : 128 * i + 128] = shifted(fdx[i])
     deep_total = dot(fkx[...], dax[...])
@@ -640,57 +698,49 @@
         o_gd[:, WIDTH * t : WIDTH * (t + 1)] = deep_total[48 * t : 48 * t + 48]
     store(o_gd, q_gd)
 
+    third_phase(0)
+
+    wait(er.at[pl.ds(1, 7)], r_e.at[0])
+    total = er[1].astype(F32)
+    for q in near[1:]:
+        total = total + er[q].astype(F32)
+    ex[x] = ep[z] + jnp.concatenate([total[:8], total[8:]], axis=1)
     for i in range(1, NX):
-        wait(ex.at[xp(-i)], r_e.at[1, i])
+        send(ex.at[x], ex.at[x], 7, r_e.at[1], **to_x(i))
+    second_phase(1)
+    wait(ex.at[pl.ds(0, 3)], r_e.at[1])
     ey[d] = (ex[0] + ex[1]) + (ex[2] + ex[3])
     for i in range(1, ND):
-        send(ey.at[d], ey.at[d], s_e.at[2, i], r_e.at[2, i], dp=dpp(i))
-
-    for i in range(1, NX):
-        wait(har.at[i], r_g.at[3, i])
-    for i in range(1, NY):
-        wait(hbr.at[i], r_g.at[4, i])
-
-    def third_step(i):
-        rows = pl.ds(pl.multiple_of(i * 48, 16), 48)
-        left_half = ha[x, rows, :].astype(F32)
-        right_half = hb[y, rows, :].astype(F32)
-        for j in range(1, 4):
-            left_half = left_half + har[j, rows, :].astype(F32)
-            right_half = right_half + hbr[j, rows, :].astype(F32)
-        zs[2 * i] = jnp.concatenate([left_half[:24], right_half[:24]], axis=0).astype(BF)
-        zs[2 * i + 1] = jnp.concatenate([left_half[24:], right_half[24:]], axis=0).astype(BF)
-
-    loop(4, third_step)
-    for i in range(1, NZ):
-        send(zs.at[zp(i)], zr.at[i], s_g.at[5, i], r_g.at[5, i], **to_z(i))
-
-    total = ey[d]
-    for i in range(1, ND):
-        wait(ey.at[dpp(-i)], r_e.at[2, i])
+        send(ey.at[d], ey.at[d], 7, r_e.at[2], dp=dpp(i))
+    third_phase(1)
+    wait(ey.at[pl.ds(0, 7)], r_e.at[2])
     total = ey[0]
     for i in range(1, ND):
         total = total + ey[i]
-    eg[z] = total
+    eg[z] = jnp.concatenate([total[:, :384], total[:, 384:]], axis=0).astype(BF)
     for i in range(1, NZ):
-        send(eg.at[z], eg.at[z], s_e.at[3, i], r_e.at[3, i], **to_z(i))
+        send(eg.at[z], eg.at[z], 7, r_e.at[3], **to_z(i))
 
     total = zs[z].astype(F32)
+    wait(zr.at[pl.ds(0, 7)], r_g.at[9])
     for i in range(1, NZ):
-        wait(zr.at[i], r_g.at[5, i])
+        total = total + zr[zp(i)].astype(F32)
+    fin[d] = total.astype(BF)
     for i in range(1, NZ):
-        total = total + zr[i].astype(F32)
-    fin[d] = total.astype(BF)
+        count(7, zs.at[i])
     for i in range(1, ND):
-        send(fin.at[d], fin.at[d], s_g.at[6, i], r_g.at[6, i], dp=dpp(i))
-    for i in range(1, NZ):
-        wait(eg.at[zp(-i)], r_e.at[3, i])
+        send(fin.at[d], fin.at[d], 7, r_g.at[10], dp=dpp(i))
+    wait(eg.at[pl.ds(0, 7)], r_e.at[3])
+    blocks = []
+    for i in range(NZ):
+        block = eg[i].astype(F32)
+        blocks.append(jnp.concatenate([block[:8], block[8:]], axis=1))
     for t in range(15):
         for j in range(4):
-            o_ge[4 * t + j : 4 * t + j + 1, :] = eg[2 * j + (15 - t) // 8, (15 - t) % 8 : (15 - t) % 8 + 1, :]
+            row = (15 - t) % 8
+            o_ge[4 * t + j : 4 * t + j + 1, :] = blocks[2 * j + (15 - t) // 8][row : row + 1, :]
     store(o_ge, q_ge)
-    for i in range(1, ND):
-        wait(fin.at[dpp(-i)], r_g.at[6, i])
+    wait(fin.at[pl.ds(0, 7)], r_g.at[10])
     for i in range(ND):
         for t in range(4):
             tile = 4 * (i // 2) + t
@@ -704,8 +754,24 @@
     out_copy.wait()
     for out in stores:
         out.wait()
-    for copy in sends:
-        copy.wait_send()
+    both = bases.at[:, pl.ds(0, 256)]
+    pltpu.make_async_copy(both, both, s_all.at[0]).wait()
+    for group in range(1, 11):
+        wait_sends(group)
+
+
+def place(*refs):
+    count = 6
+    held, sems = refs[2 * count : 3 * count], refs[-1]
+    loads = [pltpu.make_async_copy(refs[i], held[i], sems.at[0, i]) for i in range(count)]
+    stores = [pltpu.make_async_copy(held[i], refs[count + i], sems.at[1, i]) for i in range(count)]
+    for load in loads:
+        load.start()
+    for load, out in zip(loads, stores):
+        load.wait()
+        out.start()
+    for out in stores:
+        out.wait()
 
 
 def shards(bases, organism, embed_weight, conv_weight, deep_weight, human_head, mouse_head, human_cotangent, mouse_cotangent):
@@ -734,11 +800,10 @@
         vmem((NX, 192, 256), BF), vmem((NY, 192, 256), BF), vmem((4, 192, 256), BF), vmem((4, 192, 256), BF),
         vmem((NZ, 48, 256), BF), vmem((NZ, 48, 256), BF), vmem((ND, 48, 256), BF),
         vmem((EXT, WIDTH), F32), vmem((2, WIDE, WIDTH), BF),
-        vmem((NZ, 8, WIDTH), F32), vmem((NZ, 8, WIDTH), F32), vmem((NX, 8, WIDTH), F32),
-        vmem((ND, 8, WIDTH), F32), vmem((NZ, 8, WIDTH), F32),
-        dma((2,)), dma((2,)), dma((24, 8)), dma((24, 8)), dma((4, 8)), dma((4, 8)), dma((4, 8)), dma((4, 8)),
-        dma((4, 8)), dma((4, 8)), dma((4, 8)), dma((4, 8)), dma((5, 8)), dma((5, 8)), dma((7, 8)), dma((7, 8)),
-        dma((4, 8)), dma((4, 8)), dma((6,)), dma((13,)),
+        vmem((NZ, 8, WIDTH), F32), vmem((NZ, 16, 384), BF), vmem((NZ, 16, 384), BF), vmem((NX, 8, WIDTH), F32),
+        vmem((ND, 8, WIDTH), F32), vmem((NZ, 16, 384), BF),
+        dma((11,)), dma((2,)), dma((66,)), dma((8,)), dma((8,)), dma((9,)), dma((9,)), dma((5,)), dma((11,)), dma((4,)),
+        dma((6,)), dma((13,)),
     ]
     spec = pl.BlockSpec(memory_space=pl.ANY)
     ge, gc, gd, gh, gm, fd = pl.pallas_call(
@@ -762,6 +827,15 @@
         bases, organism, embed_weight, conv_weight, deep_weight,
         human_head.T, mouse_head.T, human_cotangent[0].T, mouse_cotangent[0].T,
     )
+    results = (ge, gc, gd, gh, gm, fd)
+    ge, gc, gd, gh, gm, fd = pl.pallas_call(
+        place,
+        out_shape=tuple(jax.ShapeDtypeStruct(a.shape, a.dtype) for a in results),
+        in_specs=[spec] * 6,
+        out_specs=(spec,) * 6,
+        scratch_shapes=[vmem(a.shape, a.dtype) for a in results] + [dma((2, 6))],
+        compiler_params=pltpu.CompilerParams(vmem_limit_bytes=60 * 1024 * 1024),
+    )(*results)
     return ge, gc, gd, gh.T, gm.T, fd[None]
 
 

time: 147 us -> 131 us (0.89)
  Pallas kernels: 138 us -> 130 us
  local copies, waits for them, and re-layouts: 7.96 us -> 0 us
    pallas_call x1, Pallas kernels: 138 us -> 126 us  [shards(): pl.pallas_call(kernel, out_shape=(jax.ShapeDtypeStruct((60, WIDTH), F32),...]
    unnamed x12 -> x0, local copies, waits for them, and re-layouts: 7.96 us -> none
    pallas_call x0 -> x1, Pallas kernels: none -> 3.25 us  [shards(): pl.pallas_call(place, out_shape=tuple((jax.ShapeDtypeStruct(a.shape, a.dt...]
where the time goes in v3:
time: 131 us
  Pallas kernels  130 us (99%)
  between operations  1.45 us (1%)
    pallas_call x1, Pallas kernels, shards(): pl.pallas_call(kernel, out_shape=(jax.ShapeDtypeStruct((60, WIDTH), F32),...  126 us
    pallas_call x1, Pallas kernels, shards(): pl.pallas_call(place, out_shape=tuple((jax.ShapeDtypeStruct(a.shape, a.dt...  3.25 us

profile of v3, /device:TPU:1, one launch (start us, length us, event | category | flops | bytes accessed | tf_op | source)
XLA Modules:
  0.0 131.0 jit_solution(3651502850330638111)
XLA Ops:
  1.3 126.3 %shard_map.136 = (f32[60,768]{1,0:T(8,128)}, f32[24,3840]{1,0:T(8,128)}, f32[48,3840]{1,0:T(8,128)}, f32[184,192]{1,0:T(8,128)}, f32[32,192]{1,0:T(8,128)}, /*index=5*/f32[512,768]{1,0:T(8,128)}) custom-call(s32[1,512]{1,0:T(1,128)} %i_bases.1, s32[1]{0:T(128)S(6)} %copy.15.organism, bf16[60,768]{1,0:T(8,128)(2,1)} %i_embed.1, bf16[24,3840]{1,0:T(8,128)(2,1)} %i_cw.1, ...), custom_call_target="tpu_custom_call" | custom-call | flops 10000000000 | bytes 8000000 | tf_op jit(solution)/shard_map/pallas_call | solution.py:809
  127.6 3.3 %shard_map.137 = (f32[60,768]{1,0:T(8,128)}, f32[24,3840]{1,0:T(8,128)}, f32[48,3840]{1,0:T(8,128)}, f32[184,192]{1,0:T(8,128)}, f32[32,192]{1,0:T(8,128)}, /*index=5*/f32[512,768]{1,0:T(8,128)}) custom-call(f32[60,768]{1,0:T(8,128)} %get-tuple-element.18.refs_0_, f32[24,3840]{1,0:T(8,128)} %get-tuple-element.19.refs_1_, ...), custom_call_target="tpu_custom_call" | custom-call | tf_op jit(solution)/shard_map/pallas_call | solution.py:831

commit v4 on v3

--- a/solution.py
+++ b/solution.py
@@ -18,7 +18,7 @@
 EXT = ROWS + 2 * OFF
 WIDE = 640
 HALF = 1920
-SPLIT = 1024
+SPLIT = 896
 
 SLOPE = 0.7978845608028654
 CUBIC = 0.044715
@@ -243,16 +243,16 @@
         return wg.at[zp(-q), :, :, cols]
 
     def chunk(low, h):
-        return pl.ds(pl.multiple_of(low + 256 * h, 128), 256)
+        return pl.ds(pl.multiple_of(low + 256 * h, 128), min(256, SPLIT - 256 * h))
 
     def ring0(s, h):
         for down in range(2):
-            if s == 4 and down != h // 2:
+            if s == 4 and down != 1 - h // 2:
                 continue
             q = NZ - s if down else s
             part = blk0(q, chunk(mine, h))
             wait(part, r_w.at[34 + 8 * h + q])
-            if s < 3 or (s == 3 and down == h // 2):
+            if s < 3 or (s == 3 and down == 1 - h // 2):
                 step = -1 if down else 1
                 send(part, part, 1, r_w.at[34 + 8 * h + q + step], **to_z(step))
             send(part, part, 2, r_w.at[26 + q], dp=sib)
@@ -348,7 +348,7 @@
         local.append(copy)
         send(
             acols.at[t, pl.ds(OFF, ROWS), sib_cols], ah.at[pl.ds(ROWS, ROWS), pl.ds(384 * t, 384)],
-            9, r_d.at[4], dp=sib,
+            2, r_d.at[4], dp=sib,
         )
     ah[:, pl.ds(HALF, 128)] = jnp.zeros((2 * ROWS, 128), BF)
     def conv_step(i):
@@ -544,11 +544,17 @@
         fine = (mixed[pl.ds(r0, 16), :] * row).astype(BF).astype(F32)
         fdp[pl.ds(r0 + 8, 16), :] = fine
 
-    loop(EXT // 16, fine_step, unroll=2)
     for i in range(4):
+        def fine_block(n, i=i):
+            fine_step(n + 8 * i + 1)
+
+        loop(8, fine_block, unroll=4)
         block = fdp[OFF + 8 + 128 * i : OFF + 136 + 128 * i, :]
         fdt[0, :, 128 * i : 128 * i + 128] = block.T.astype(BF)
-    send(fdt.at[0], fdt.at[1], 6, r_g.at[0], dp=sib)
+        part = fdt.at[:, :, pl.ds(128 * i, 128)]
+        send(part.at[0], part.at[1], 6, r_g.at[0], dp=sib)
+    fine_step(0)
+    fine_step(EXT // 16 - 1)
 
     def back_shift(i):
         r0 = pl.multiple_of(i * 32, 32)
@@ -571,7 +577,8 @@
             [total[24 * (4 * zz + xx) : 24 * (4 * zz + xx) + 24] for zz in range(NZ)], axis=0
         ).astype(BF)
 
-    halves = (pl.ds(0, 96), pl.ds(96, 96))
+    halves = (pl.ds(0, 144), pl.ds(144, 48))
+    pairs = (range(3), range(3, 4))
 
     def alpha_send(i, h):
         send(
@@ -606,8 +613,8 @@
     def second_phase(h):
         wait(gar.at[pl.ds(1, 3), :, halves[h]], r_g.at[1 + h])
         for xx in range(NX):
-            for low in (96 * h, 96 * h + 48):
-                rows = pl.ds(low, 48)
+            for m in pairs[h]:
+                rows = pl.ds(48 * m, 48)
                 total = ga[y, xx, rows, :].astype(F32)
                 for i in range(1, NY):
                     total = total + gar[i, xx, rows, :].astype(F32)
@@ -616,8 +623,8 @@
             send(ha.at[xp(i), halves[h]], har.at[i, halves[h]], 7, r_g.at[5 + h], **to_x(i))
         wait(gbr.at[pl.ds(1, 3), :, halves[h]], r_g.at[3 + h])
         for yy in range(NY):
-            for low in (96 * h, 96 * h + 48):
-                rows = pl.ds(low, 48)
+            for m in pairs[h]:
+                rows = pl.ds(48 * m, 48)
                 total = gb[x, yy, rows, :].astype(F32)
                 for i in range(1, NX):
                     total = total + gbr[i, yy, rows, :].astype(F32)
@@ -637,14 +644,14 @@
     def third_phase(h):
         wait(har.at[pl.ds(1, 3), halves[h]], r_g.at[5 + h])
         wait(hbr.at[pl.ds(1, 3), halves[h]], r_g.at[7 + h])
-        for m in range(2):
-            rows = pl.ds(96 * h + 48 * m, 48)
+        for m in pairs[h]:
+            rows = pl.ds(48 * m, 48)
             left_half = ha[x, rows, :].astype(F32)
             right_half = hb[y, rows, :].astype(F32)
             for i in range(1, 4):
                 left_half = left_half + har[i, rows, :].astype(F32)
                 right_half = right_half + hbr[i, rows, :].astype(F32)
-            zz = 4 * h + 2 * m
+            zz = 2 * m
             zs[zz] = jnp.concatenate([left_half[:24], right_half[:24]], axis=0).astype(BF)
             zs[zz + 1] = jnp.concatenate([left_half[24:], right_half[24:]], axis=0).astype(BF)
             for to in (zz, zz + 1):
@@ -663,7 +670,6 @@
     for i in range(3):
         back_step(i)
 
-    second_phase(0)
     fhl[0, EXT:WIDE, :] = jnp.zeros((WIDE - EXT, WIDTH), BF)
     fhl[1, EXT:WIDE, :] = jnp.zeros((WIDE - EXT, WIDTH), BF)
 
@@ -689,6 +695,8 @@
         es[q] = jnp.concatenate([part[:, :384], part[:, 384:]], axis=0).astype(BF)
         send(es.at[q], er.at[q], 7, r_e.at[0], **to_z(q))
 
+    second_phase(0)
+
     wait(dax.at[pl.ds(0, 896)], r_d.at[0])
     wait(fdx.at[pl.ds(0, 7)], r_d.at[3])
     for i in range(ND):
@@ -698,8 +706,6 @@
         o_gd[:, WIDTH * t : WIDTH * (t + 1)] = deep_total[48 * t : 48 * t + 48]
     store(o_gd, q_gd)
 
-    third_phase(0)
-
     wait(er.at[pl.ds(1, 7)], r_e.at[0])
     total = er[1].astype(F32)
     for q in near[1:]:
@@ -708,6 +714,7 @@
     for i in range(1, NX):
         send(ex.at[x], ex.at[x], 7, r_e.at[1], **to_x(i))
     second_phase(1)
+    third_phase(0)
     wait(ex.at[pl.ds(0, 3)], r_e.at[1])
     ey[d] = (ex[0] + ex[1]) + (ex[2] + ex[3])
     for i in range(1, ND):
@@ -763,8 +770,14 @@
 def place(*refs):
     count = 6
     held, sems = refs[2 * count : 3 * count], refs[-1]
-    loads = [pltpu.make_async_copy(refs[i], held[i], sems.at[0, i]) for i in range(count)]
-    stores = [pltpu.make_async_copy(held[i], refs[count + i], sems.at[1, i]) for i in range(count)]
+    pieces = []
+    for i, size in ((5, 128), (2, 24), (1, 24), (0, 60), (3, 184), (4, 32)):
+        for low in range(0, held[i].shape[0], size):
+            pieces.append((i, pl.ds(low, size)))
+    loads, stores = [], []
+    for n, (i, rows) in enumerate(pieces):
+        loads.append(pltpu.make_async_copy(refs[i].at[rows], held[i].at[rows], sems.at[0, n]))
+        stores.append(pltpu.make_async_copy(held[i].at[rows], refs[count + i].at[rows], sems.at[1, n]))
     for load in loads:
         load.start()
     for load, out in zip(loads, stores):
@@ -833,7 +846,7 @@
         out_shape=tuple(jax.ShapeDtypeStruct(a.shape, a.dtype) for a in results),
         in_specs=[spec] * 6,
         out_specs=(spec,) * 6,
-        scratch_shapes=[vmem(a.shape, a.dtype) for a in results] + [dma((2, 6))],
+        scratch_shapes=[vmem(a.shape, a.dtype) for a in results] + [dma((2, 10))],
         compiler_params=pltpu.CompilerParams(vmem_limit_bytes=60 * 1024 * 1024),
     )(*results)
     return ge, gc, gd, gh.T, gm.T, fd[None]

time: 131 us -> 126 us (0.962)
  Pallas kernels: 130 us -> 125 us
    pallas_call x1, Pallas kernels: 126 us -> 122 us  [shards(): pl.pallas_call(kernel, out_shape=(jax.ShapeDtypeStruct((60, WIDTH), F32),...]
where the time goes in v4:
time: 126 us
  Pallas kernels  125 us (99%)
  between operations  1.45 us (1%)
    pallas_call x1, Pallas kernels, shards(): pl.pallas_call(kernel, out_shape=(jax.ShapeDtypeStruct((60, WIDTH), F32),...  122 us
    pallas_call x1, Pallas kernels, shards(): pl.pallas_call(place, out_shape=tuple((jax.ShapeDtypeStruct(a.shape, a.dt...  2.8 us

profile of v4, /device:TPU:1, one launch (start us, length us, event | category | flops | bytes accessed | tf_op | source)
XLA Modules:
  0.0 126.2 jit_solution(5645966123580492580)
XLA Ops:
  1.3 122.0 %shard_map.136 = (f32[60,768]{1,0:T(8,128)}, f32[24,3840]{1,0:T(8,128)}, f32[48,3840]{1,0:T(8,128)}, f32[184,192]{1,0:T(8,128)}, f32[32,192]{1,0:T(8,128)}, /*index=5*/f32[512,768]{1,0:T(8,128)}) custom-call(s32[1,512]{1,0:T(1,128)} %i_bases.1, s32[1]{0:T(128)S(6)} %copy.15.organism, bf16[60,768]{1,0:T(8,128)(2,1)} %i_embed.1, bf16[24,3840]{1,0:T(8,128)(2,1)} %i_cw.1, ...), custom_call_target="tpu_custom_call" | custom-call | flops 10000000000 | bytes 8000000 | tf_op jit(solution)/shard_map/pallas_call | solution.py:822
  123.3 2.8 %shard_map.137 = (f32[60,768]{1,0:T(8,128)}, f32[24,3840]{1,0:T(8,128)}, f32[48,3840]{1,0:T(8,128)}, f32[184,192]{1,0:T(8,128)}, f32[32,192]{1,0:T(8,128)}, /*index=5*/f32[512,768]{1,0:T(8,128)}) custom-call(f32[60,768]{1,0:T(8,128)} %get-tuple-element.18.refs_0_, f32[24,3840]{1,0:T(8,128)} %get-tuple-element.19.refs_1_, ...), custom_call_target="tpu_custom_call" | custom-call | tf_op jit(solution)/shard_map/pallas_call | solution.py:844

commit v5 on v4

--- a/solution.py
+++ b/solution.py
@@ -358,7 +358,7 @@
             total = total + dot(acols[t], wf[pl.ds(o0_, 256), WIDTH * t : WIDTH * (t + 1)], 1, 1)
         mixed[:, pl.ds(o0_, 256)] = total
 
-    loop(3, conv_step)
+    loop(3, conv_step, unroll=3)
 
     pooled = []
     for t in range(4):
@@ -710,21 +710,25 @@
     total = er[1].astype(F32)
     for q in near[1:]:
         total = total + er[q].astype(F32)
-    ex[x] = ep[z] + jnp.concatenate([total[:8], total[8:]], axis=1)
+    own = ep[z]
+    ex[x] = (total + jnp.concatenate([own[:, :384], own[:, 384:]], axis=0)).astype(BF)
     for i in range(1, NX):
         send(ex.at[x], ex.at[x], 7, r_e.at[1], **to_x(i))
     second_phase(1)
     third_phase(0)
     wait(ex.at[pl.ds(0, 3)], r_e.at[1])
-    ey[d] = (ex[0] + ex[1]) + (ex[2] + ex[3])
+    total = ex[0].astype(F32)
+    for i in range(1, NX):
+        total = total + ex[i].astype(F32)
+    ey[d] = total.astype(BF)
     for i in range(1, ND):
         send(ey.at[d], ey.at[d], 7, r_e.at[2], dp=dpp(i))
     third_phase(1)
     wait(ey.at[pl.ds(0, 7)], r_e.at[2])
-    total = ey[0]
+    total = ey[0].astype(F32)
     for i in range(1, ND):
-        total = total + ey[i]
-    eg[z] = jnp.concatenate([total[:, :384], total[:, 384:]], axis=0).astype(BF)
+        total = total + ey[i].astype(F32)
+    eg[z] = total.astype(BF)
     for i in range(1, NZ):
         send(eg.at[z], eg.at[z], 7, r_e.at[3], **to_z(i))
 
@@ -813,8 +817,8 @@
         vmem((NX, 192, 256), BF), vmem((NY, 192, 256), BF), vmem((4, 192, 256), BF), vmem((4, 192, 256), BF),
         vmem((NZ, 48, 256), BF), vmem((NZ, 48, 256), BF), vmem((ND, 48, 256), BF),
         vmem((EXT, WIDTH), F32), vmem((2, WIDE, WIDTH), BF),
-        vmem((NZ, 8, WIDTH), F32), vmem((NZ, 16, 384), BF), vmem((NZ, 16, 384), BF), vmem((NX, 8, WIDTH), F32),
-        vmem((ND, 8, WIDTH), F32), vmem((NZ, 16, 384), BF),
+        vmem((NZ, 8, WIDTH), F32), vmem((NZ, 16, 384), BF), vmem((NZ, 16, 384), BF), vmem((NX, 16, 384), BF),
+        vmem((ND, 16, 384), BF), vmem((NZ, 16, 384), BF),
         dma((11,)), dma((2,)), dma((66,)), dma((8,)), dma((8,)), dma((9,)), dma((9,)), dma((5,)), dma((11,)), dma((4,)),
         dma((6,)), dma((13,)),
     ]

time: 126 us -> 127 us (level)
  no operation moved by 1% of the time
where the time goes in v5:
time: 127 us
  Pallas kernels  125 us (98%)
  between operations  1.45 us (1%)
    pallas_call x1, Pallas kernels, shards(): pl.pallas_call(kernel, out_shape=(jax.ShapeDtypeStruct((60, WIDTH), F32),...  123 us
    pallas_call x1, Pallas kernels, shards(): pl.pallas_call(place, out_shape=tuple((jax.ShapeDtypeStruct(a.shape, a.dt...  2.8 us

profile of v5, /device:TPU:1, one launch (start us, length us, event | category | flops | bytes accessed | tf_op | source)
XLA Modules:
  0.0 126.8 jit_solution(8562519352404173897)
XLA Ops:
  1.3 122.5 %shard_map.136 = (f32[60,768]{1,0:T(8,128)}, f32[24,3840]{1,0:T(8,128)}, f32[48,3840]{1,0:T(8,128)}, f32[184,192]{1,0:T(8,128)}, f32[32,192]{1,0:T(8,128)}, /*index=5*/f32[512,768]{1,0:T(8,128)}) custom-call(s32[1,512]{1,0:T(1,128)} %i_bases.1, s32[1]{0:T(128)S(6)} %copy.15.organism, bf16[60,768]{1,0:T(8,128)(2,1)} %i_embed.1, bf16[24,3840]{1,0:T(8,128)(2,1)} %i_cw.1, ...), custom_call_target="tpu_custom_call" | custom-call | flops 10000000000 | bytes 8000000 | tf_op jit(solution)/shard_map/pallas_call | solution.py:826
  123.8 2.8 %shard_map.137 = (f32[60,768]{1,0:T(8,128)}, f32[24,3840]{1,0:T(8,128)}, f32[48,3840]{1,0:T(8,128)}, f32[184,192]{1,0:T(8,128)}, f32[32,192]{1,0:T(8,128)}, /*index=5*/f32[512,768]{1,0:T(8,128)}) custom-call(f32[60,768]{1,0:T(8,128)} %get-tuple-element.18.refs_0_, f32[24,3840]{1,0:T(8,128)} %get-tuple-element.19.refs_1_, ...), custom_call_target="tpu_custom_call" | custom-call | tf_op jit(solution)/shard_map/pallas_call | solution.py:848
